TPU v7x, 32 devices: a whole 2x2x4 slice. The times are simulated.
32 devices in a mesh: seq: 4 (over z), shard: 8 (over y, x, core).
Axes of the slice: x: 2, y: 2, z: 4, core: 2. Of those that a mesh axis runs over, the one named last changes fastest.
Arguments:
- tokens: bfloat16 [8, 2048, 768], P('shard', 'seq'), may hold values from -6 to 6
- ln1_gain: bfloat16 [768], P('shard'), may hold values from 0.099609375 to 1.8984375
- ln1_shift: bfloat16 [768], P('shard'), may hold values from -3 to 3
- w_qkv: bfloat16 [768, 2304], P('shard'), may hold values from -0.21875 to 0.21875
- q_bias: bfloat16 [768], P('shard'), may hold values from -3 to 3
- v_bias: bfloat16 [768], P('shard'), may hold values from -3 to 3
- w_out: bfloat16 [768, 768], P('shard'), may hold values from -3 to 3
- out_bias: bfloat16 [768], P('shard'), may hold values from -3 to 3
- ln2_gain: bfloat16 [768], P('shard'), may hold values from 0.099609375 to 1.8984375
- ln2_shift: bfloat16 [768], P('shard'), may hold values from -3 to 3
- w_in: bfloat16 [768, 3072], P('shard'), may hold values from -0.21875 to 0.21875
- in_bias: bfloat16 [3072], P('shard'), may hold values from -3 to 3
- w_fin: bfloat16 [3072, 768], P('shard'), may hold values from -0.109375 to 0.109375
- fin_bias: bfloat16 [768], P('shard'), may hold values from -3 to 3
- cotangent: bfloat16 [8, 2048, 768], P('shard', 'seq'), may hold values from -6 to 6
- lengths: int32 [8], P('shard'), may hold values from 512 to 2048, as said below
Outputs:
- output: bfloat16 [8, 2048, 768], P('shard', 'seq')
- grad_tokens: bfloat16 [8, 2048, 768], P('shard', 'seq')
- grad_ln1_gain: float32 [768], P('shard')
- grad_ln1_shift: float32 [768], P('shard')
- grad_w_qkv: float32 [768, 2304], P('shard')
- grad_q_bias: float32 [768], P('shard')
- grad_v_bias: float32 [768], P('shard')
- grad_w_out: float32 [768, 768], P('shard')
- grad_out_bias: float32 [768], P('shard')
- grad_ln2_gain: float32 [768], P('shard')
- grad_ln2_shift: float32 [768], P('shard')
- grad_w_in: float32 [768, 3072], P('shard')
- grad_in_bias: float32 [3072], P('shard')
- grad_w_fin: float32 [3072, 768], P('shard')
- grad_fin_bias: float32 [768], P('shard')
Inputs may be any that keep to these rules, and one draw needn't show every extreme that they name: Each slot holds lengths[s] valid tokens at its start; at least one slot is full, with 2048.
All inputs are finite; a program needn't handle non-finite values.
Results may differ from a plain program's by a relative error of at most 0.014.
Values may be sent and summed in bfloat16 or wider, within the bound.
A program may use at most 128 MiB of HBM per device.

v0:
```python
import jax
import jax.numpy as jnp
from jax import lax
from jax.sharding import PartitionSpec as P

HEAD_DIM = 64


EPS = 1e-05
GELU_C = 0.7978845608028654
GELU_K = 0.044715


def gelu_slope(values):
    swing = jnp.tanh(GELU_C * (values + GELU_K * values * values * values))
    return 0.5 * (1.0 + swing) + 0.5 * values * (1.0 - swing * swing) * GELU_C * (
        1.0 + 3.0 * GELU_K * values * values
    )


def norm_parts(values, gain, shift):
    average = jnp.mean(values, -1, keepdims=True)
    centred = values - average
    inverse = lax.rsqrt(jnp.mean(centred * centred, -1, keepdims=True) + EPS)
    unit = centred * inverse
    return (unit * gain + shift, unit, inverse)


def norm_back(grad_out, unit, inverse, gain):
    grad_unit = grad_out * gain
    grad_in = inverse * (
        grad_unit
        - jnp.mean(grad_unit, -1, keepdims=True)
        - unit * jnp.mean(grad_unit * unit, -1, keepdims=True)
    )
    return (grad_in, jnp.sum(grad_out * unit, 0), jnp.sum(grad_out, 0))


def contract_rows(left, right):
    return lax.dot_general(
        left, right, (((0,), (0,)), ((), ())), preferred_element_type=jnp.float32
    )


def contract_cols(left, right):
    return lax.dot_general(
        left, right, (((1,), (1,)), ((), ())), preferred_element_type=jnp.float32
    )


def split_packed(packed):
    slot_len = packed.shape[0]
    heads = packed.shape[2] // HEAD_DIM
    query = packed[:, 0].reshape(slot_len, heads, HEAD_DIM)
    keys = packed[:, 1].reshape(slot_len, heads, HEAD_DIM)
    values = packed[:, 2].reshape(slot_len, heads, HEAD_DIM)
    return (query, keys, values)


def attend_slot(packed, length, row_block, scale):
    slot_len, group = (packed.shape[0], packed.shape[2])
    query, keys, values = split_packed(packed)
    heads = group // HEAD_DIM
    key_live = jnp.arange(slot_len, dtype=jnp.int32) < length

    def one_block(query_rows):
        scores = (
            jnp.einsum("qhd,khd->hqk", query_rows, keys, preferred_element_type=jnp.float32) * scale
        )
        scores = jnp.where(key_live[None, None, :], scores, -jnp.inf)
        highest = jnp.max(scores, -1, keepdims=True)
        raised = jnp.exp(scores - highest)
        total = jnp.sum(raised, -1, keepdims=True)
        weights = (raised / total).astype(jnp.bfloat16)
        context = jnp.einsum("hqk,khd->qhd", weights, values, preferred_element_type=jnp.float32)
        return (
            context.astype(jnp.bfloat16).reshape(row_block, group),
            (highest + jnp.log(total))[..., 0],
        )

    blocked = query.reshape(slot_len // row_block, row_block, heads, HEAD_DIM)
    context, log_total = lax.map(one_block, blocked)
    return (context.reshape(slot_len, group), log_total)


def attend_back(packed, grad_context, log_total, length, row_block, scale):
    slot_len, group = (packed.shape[0], packed.shape[2])
    query, keys, values = split_packed(packed)
    heads = group // HEAD_DIM
    key_live = jnp.arange(slot_len, dtype=jnp.int32) < length
    blocks = slot_len // row_block

    def one_block(carry, inputs):
        grad_keys, grad_values = carry
        query_rows, grad_rows, log_rows = inputs
        scores = (
            jnp.einsum("qhd,khd->hqk", query_rows, keys, preferred_element_type=jnp.float32) * scale
        )
        scores = jnp.where(key_live[None, None, :], scores, -jnp.inf)
        weights = jnp.exp(scores - log_rows[..., None])
        grad_values = grad_values + jnp.einsum(
            "hqk,qhd->khd",
            weights.astype(jnp.bfloat16),
            grad_rows,
            preferred_element_type=jnp.float32,
        )
        grad_weights = jnp.einsum(
            "qhd,khd->hqk", grad_rows, values, preferred_element_type=jnp.float32
        )
        inner_sum = jnp.sum(weights * grad_weights, -1, keepdims=True)
        grad_scores = (weights * (grad_weights - inner_sum)).astype(jnp.bfloat16)
        grad_query = (
            jnp.einsum("hqk,khd->qhd", grad_scores, keys, preferred_element_type=jnp.float32)
            * scale
        ).astype(jnp.bfloat16)
        grad_keys = (
            grad_keys
            + jnp.einsum(
                "hqk,qhd->khd", grad_scores, query_rows, preferred_element_type=jnp.float32
            )
            * scale
        )
        return ((grad_keys, grad_values), grad_query)

    empty = jnp.zeros((slot_len, heads, HEAD_DIM), jnp.float32)
    inputs = (
        query.reshape(blocks, row_block, heads, HEAD_DIM),
        grad_context.reshape(blocks, row_block, heads, HEAD_DIM),
        log_total,
    )
    (grad_keys, grad_values), grad_query = lax.scan(one_block, (empty, empty), inputs)
    return jnp.stack(
        (
            grad_query.reshape(slot_len, group),
            grad_keys.astype(jnp.bfloat16).reshape(slot_len, group),
            grad_values.astype(jnp.bfloat16).reshape(slot_len, group),
        ),
        1,
    )


def on_device(
    tokens,
    ln1_gain,
    ln1_shift,
    w_qkv,
    q_bias,
    v_bias,
    w_out,
    out_bias,
    ln2_gain,
    ln2_shift,
    w_in,
    in_bias,
    w_fin,
    fin_bias,
    cotangent,
    lengths,
):
    slots_here, local_len, width = tokens.shape
    slot_len = local_len * lax.axis_size("seq")
    row_block = min(512, slot_len)
    scale = HEAD_DIM ** (-0.5)
    (
        full_ln1_gain,
        full_ln1_shift,
        full_w_qkv,
        full_q_bias,
        full_v_bias,
        full_w_out,
        full_out_bias,
        full_ln2_gain,
        full_ln2_shift,
        full_w_in,
        full_in_bias,
        full_w_fin,
        full_fin_bias,
    ) = (
        lax.all_gather(ln1_gain, "shard", axis=0, tiled=True),
        lax.all_gather(ln1_shift, "shard", axis=0, tiled=True),
        lax.all_gather(w_qkv, "shard", axis=0, tiled=True),
        lax.all_gather(q_bias, "shard", axis=0, tiled=True),
        lax.all_gather(v_bias, "shard", axis=0, tiled=True),
        lax.all_gather(w_out, "shard", axis=0, tiled=True),
        lax.all_gather(out_bias, "shard", axis=0, tiled=True),
        lax.all_gather(ln2_gain, "shard", axis=0, tiled=True),
        lax.all_gather(ln2_shift, "shard", axis=0, tiled=True),
        lax.all_gather(w_in, "shard", axis=0, tiled=True),
        lax.all_gather(in_bias, "shard", axis=0, tiled=True),
        lax.all_gather(w_fin, "shard", axis=0, tiled=True),
        lax.all_gather(fin_bias, "shard", axis=0, tiled=True),
    )
    inputs = tokens.reshape(-1, width).astype(jnp.float32)
    normed_one, unit_one, inverse_one = norm_parts(
        inputs, full_ln1_gain.astype(jnp.float32), full_ln1_shift.astype(jnp.float32)
    )
    normed_one = normed_one.astype(jnp.bfloat16)
    qkv_bias = jnp.concatenate(
        (
            full_q_bias.astype(jnp.float32),
            jnp.zeros((width,), jnp.float32),
            full_v_bias.astype(jnp.float32),
        )
    )
    projected = (
        jnp.dot(normed_one, full_w_qkv, preferred_element_type=jnp.float32) + qkv_bias
    ).astype(jnp.bfloat16)
    packed = lax.all_to_all(
        projected.reshape(slots_here, local_len, 3, width),
        "seq",
        split_axis=3,
        concat_axis=1,
        tiled=True,
    )
    context_heads, log_total = lax.map(
        lambda inputs_pair: attend_slot(inputs_pair[0], inputs_pair[1], row_block, scale),
        (packed, lengths),
    )
    context = lax.all_to_all(context_heads, "seq", split_axis=1, concat_axis=2, tiled=True).reshape(
        -1, width
    )
    branch = jnp.dot(
        context, full_w_out, preferred_element_type=jnp.float32
    ) + full_out_bias.astype(jnp.float32)
    middle = inputs + branch
    normed_two, unit_two, inverse_two = norm_parts(
        middle, full_ln2_gain.astype(jnp.float32), full_ln2_shift.astype(jnp.float32)
    )
    normed_two = normed_two.astype(jnp.bfloat16)
    inner = jnp.dot(
        normed_two, full_w_in, preferred_element_type=jnp.float32
    ) + full_in_bias.astype(jnp.float32)
    active = jax.nn.gelu(inner, approximate=True).astype(jnp.bfloat16)
    output = (
        middle
        + jnp.dot(active, full_w_fin, preferred_element_type=jnp.float32)
        + full_fin_bias.astype(jnp.float32)
    )
    result = output.astype(jnp.bfloat16).reshape(tokens.shape)
    positions = lax.axis_index("seq") * local_len + jnp.arange(local_len, dtype=jnp.int32)
    live = (positions[None, :] < lengths[:, None]).astype(jnp.float32)
    grad_output = (cotangent.astype(jnp.float32) * live[:, :, None]).reshape(-1, width)
    back_gain_one, back_w_qkv, back_w_out, back_gain_two, back_w_in, back_w_fin = (
        lax.all_gather(ln1_gain, "shard", axis=0, tiled=True),
        lax.all_gather(w_qkv, "shard", axis=0, tiled=True),
        lax.all_gather(w_out, "shard", axis=0, tiled=True),
        lax.all_gather(ln2_gain, "shard", axis=0, tiled=True),
        lax.all_gather(w_in, "shard", axis=0, tiled=True),
        lax.all_gather(w_fin, "shard", axis=0, tiled=True),
    )
    grad_outer = grad_output.astype(jnp.bfloat16)
    grad_fin_bias = jnp.sum(grad_outer.astype(jnp.float32), 0)
    grad_w_fin = contract_rows(active, grad_outer)
    grad_active = contract_cols(grad_outer, back_w_fin)
    grad_inner = (grad_active * gelu_slope(inner)).astype(jnp.bfloat16)
    grad_in_bias = jnp.sum(grad_inner.astype(jnp.float32), 0)
    grad_w_in = contract_rows(normed_two, grad_inner)
    grad_normed_two = contract_cols(grad_inner, back_w_in)
    grad_norm_two, grad_ln2_gain, grad_ln2_shift = norm_back(
        grad_normed_two, unit_two, inverse_two, back_gain_two.astype(jnp.float32)
    )
    grad_middle = grad_output + grad_norm_two
    grad_branch = grad_middle.astype(jnp.bfloat16)
    grad_out_bias = jnp.sum(grad_branch.astype(jnp.float32), 0)
    grad_w_out = contract_rows(context, grad_branch)
    grad_context = contract_cols(grad_branch, back_w_out).astype(jnp.bfloat16)
    grad_heads = lax.all_to_all(
        grad_context.reshape(slots_here, local_len, width),
        "seq",
        split_axis=2,
        concat_axis=1,
        tiled=True,
    )
    grad_packed = lax.map(
        lambda inputs_four: attend_back(
            inputs_four[0], inputs_four[1], inputs_four[2], inputs_four[3], row_block, scale
        ),
        (packed, grad_heads, log_total, lengths),
    )
    grad_projected = lax.all_to_all(
        grad_packed, "seq", split_axis=1, concat_axis=3, tiled=True
    ).reshape(-1, 3 * width)
    grad_q_bias = jnp.sum(grad_projected[:, :width].astype(jnp.float32), 0)
    grad_v_bias = jnp.sum(grad_projected[:, 2 * width :].astype(jnp.float32), 0)
    grad_w_qkv = contract_rows(normed_one, grad_projected)
    grad_normed_one = contract_cols(grad_projected, back_w_qkv)
    grad_norm_one, grad_ln1_gain, grad_ln1_shift = norm_back(
        grad_normed_one, unit_one, inverse_one, back_gain_one.astype(jnp.float32)
    )
    grad_tokens = (grad_middle + grad_norm_one).astype(jnp.bfloat16).reshape(tokens.shape)
    every_share = (
        lax.psum_scatter(grad_ln1_gain, "shard", scatter_dimension=0, tiled=True),
        lax.psum_scatter(grad_ln1_shift, "shard", scatter_dimension=0, tiled=True),
        lax.psum_scatter(grad_w_qkv, "shard", scatter_dimension=0, tiled=True),
        lax.psum_scatter(grad_q_bias, "shard", scatter_dimension=0, tiled=True),
        lax.psum_scatter(grad_v_bias, "shard", scatter_dimension=0, tiled=True),
        lax.psum_scatter(grad_w_out, "shard", scatter_dimension=0, tiled=True),
        lax.psum_scatter(grad_out_bias, "shard", scatter_dimension=0, tiled=True),
        lax.psum_scatter(grad_ln2_gain, "shard", scatter_dimension=0, tiled=True),
        lax.psum_scatter(grad_ln2_shift, "shard", scatter_dimension=0, tiled=True),
        lax.psum_scatter(grad_w_in, "shard", scatter_dimension=0, tiled=True),
        lax.psum_scatter(grad_in_bias, "shard", scatter_dimension=0, tiled=True),
        lax.psum_scatter(grad_w_fin, "shard", scatter_dimension=0, tiled=True),
        lax.psum_scatter(grad_fin_bias, "shard", scatter_dimension=0, tiled=True),
    )
    (
        total_ln1_gain,
        total_ln1_shift,
        total_w_qkv,
        total_q_bias,
        total_v_bias,
        total_w_out,
        total_out_bias,
        total_ln2_gain,
        total_ln2_shift,
        total_w_in,
        total_in_bias,
        total_w_fin,
        total_fin_bias,
    ) = (
        lax.psum(every_share[0].astype(jnp.bfloat16), "seq").astype(jnp.float32),
        lax.psum(every_share[1].astype(jnp.bfloat16), "seq").astype(jnp.float32),
        lax.psum(every_share[2].astype(jnp.bfloat16), "seq").astype(jnp.float32),
        lax.psum(every_share[3].astype(jnp.bfloat16), "seq").astype(jnp.float32),
        lax.psum(every_share[4].astype(jnp.bfloat16), "seq").astype(jnp.float32),
        lax.psum(every_share[5].astype(jnp.bfloat16), "seq").astype(jnp.float32),
        lax.psum(every_share[6].astype(jnp.bfloat16), "seq").astype(jnp.float32),
        lax.psum(every_share[7].astype(jnp.bfloat16), "seq").astype(jnp.float32),
        lax.psum(every_share[8].astype(jnp.bfloat16), "seq").astype(jnp.float32),
        lax.psum(every_share[9].astype(jnp.bfloat16), "seq").astype(jnp.float32),
        lax.psum(every_share[10].astype(jnp.bfloat16), "seq").astype(jnp.float32),
        lax.psum(every_share[11].astype(jnp.bfloat16), "seq").astype(jnp.float32),
        lax.psum(every_share[12].astype(jnp.bfloat16), "seq").astype(jnp.float32),
    )
    return (
        result,
        grad_tokens,
        total_ln1_gain,
        total_ln1_shift,
        total_w_qkv,
        total_q_bias,
        total_v_bias,
        total_w_out,
        total_out_bias,
        total_ln2_gain,
        total_ln2_shift,
        total_w_in,
        total_in_bias,
        total_w_fin,
        total_fin_bias,
    )


def solution(mesh):
    return jax.shard_map(
        on_device,
        mesh=mesh,
        in_specs=(
            P("shard", "seq", None),
            P("shard"),
            P("shard"),
            P("shard", None),
            P("shard"),
            P("shard"),
            P("shard", None),
            P("shard"),
            P("shard"),
            P("shard"),
            P("shard", None),
            P("shard"),
            P("shard", None),
            P("shard"),
            P("shard", "seq", None),
            P("shard"),
        ),
        out_specs=(
            P("shard", "seq", None),
            P("shard", "seq", None),
            P("shard"),
            P("shard"),
            P("shard", None),
            P("shard"),
            P("shard"),
            P("shard", None),
            P("shard"),
            P("shard"),
            P("shard"),
            P("shard", None),
            P("shard"),
            P("shard", None),
            P("shard"),
        ),
        check_vma=False,
    )
```

profile of v0, /device:TPU:1, one launch (start us, length us, event | category | flops | bytes accessed | tf_op | source)
XLA Modules:
  0.0 709.9 jit_solution(14129866419527028276)
XLA Ops:
  18.1 22.7 %all-reduce.18 = (bf16[768]{0:T(1024)(128)(2,1)S(1)}, bf16[768]{0:T(1024)(128)(2,1)S(1)}, bf16[768]{0:T(1024)(128)(2,1)S(1)}, bf16[768]{0:T(1024)(128)(2,1)S(1)}...) all-reduce(bf16[768]{0:T(1024)(128)(2,1)S(1)} %dynamic-update-slice, ...), channel_id=1, replica_groups=mesh['seq'=4,'shard'=8] {'shard'}, use_global_device_ids=true, to_apply=%add.3 | all-reduce | flops 6144 | bytes 24576
  42.6 4.0 all-gather.6.cloned.1.call-done
  46.6 5.6 fusion.60
  55.0 3.7 copy.62
  58.7 4.3 all-to-all-start
  63.6 69.6 %all-to-all-done = bf16[1,512,3,768]{1,2,0,3:T(4,128)(2,1)S(1)} async-done(((bf16[1,512,3,768]{1,2,0,3:T(4,128)(2,1)}), bf16[1,512,3,768]{1,2,0,3:T(4,128)(2,1)S(1)}, u32[]{:S(2)}, u32[]{:S(2)}) %all-to-all-start) | async-done | bytes 2359328 | tf_op jit(solution)/shard_map/all_to_all | solution.py:208
  141.1 39.2 %while.46 = (s32[]{:T(128)}, bf16[4,512,192]{1,2,0:T(8,128)(2,1)}, f32[4,3,512]{2,1,0:T(4,128)S(1)}, bf16[4,512,3,64]{1,3,2,0:T(8,128)(2,1)S(1)}, bf16[2048,3,64...) while((s32[]{:T(128)}, bf16[4,512,192]{1,2,0:T(8,128)(2,1)}, ...), condition=%wide.region_5.6_spmd.clone, body=%wide.region_2.5_spmd.clone.sunk | while | flops 843153920 | bytes 40171628 | solution.py:82
  156.4 3.6 fusion.152
  166.2 3.6 fusion.152
  176.0 3.6 fusion.152
  185.7 12.7 %reduce.1 = bf16[2048,192]{1,0:T(8,128)(2,1)S(1)} reduce(bf16[2048,1,192]{2,1,0:T(2,128)(2,1)} %bitcast.200, bf16[]{:T(256)} %broadcast.226), dimensions={1}, to_apply=%bitcast.122.reduce_sub_computation | reduce | bytes 1572866
  205.0 10.5 %all-gather = bf16[8,1,384]{2,1,0:T(2,128)(2,1)S(1)} all-gather(bf16[1,1,384]{2,1,0:T(2,128)(2,1)S(1)} %reshape.231), channel_id=1, replica_groups=mesh['seq'=4,'shard'=8] {'shard'}, dimensions={0}, use_global_device_ids=true | all-gather | bytes 6912 | tf_op jit(solution)/shard_map/all_gather | solution.py:189
  215.5 8.3 %all-to-all-done.1 = bf16[4,2,49152]{2,1,0:T(2,128)(2,1)S(1)} async-done(((bf16[4,2,49152]{2,1,0:T(2,128)(2,1)}), bf16[4,2,49152]{2,1,0:T(2,128)(2,1)S(1)}, u32[]{:S(2)}, u32[]{:S(2)}) %all-to-all-start.1) | async-done | bytes 786464 | tf_op jit(solution)/shard_map/all_to_all | solution.py:219
  226.4 4.6 copy.68
  237.7 8.3 %fusion.103 = f32[512,3072]{1,0:T(8,128)} fusion(bf16[768,3072]{1,0:T(8,128)(2,1)} %all-gather.10.cloned.1.call-done, f32[512,768]{1,0:T(8,128)} %copy-done.9, f32[768]{0:T(1024)S(1)} %convert_element_type.215, f32[768]{0:T(1024)S(1)} %convert_element_type.214, f32[512]{0:T(512)S(1)} %add_rsqrt_fusion, f32[512]{0:T(512)S(1)} %broadcast_multiply_fusion.4), kind=kOutput, calls=%fused_computation.151 | convolution fusion | flops 2417885184 | bytes 12593152 | tf_op jit(solution)/shard_map/dot_general | solution.py:230
  246.0 9.5 %convert_reduce_fusion = (f32[3072]{0:T(1024)}, bf16[512,3072]{1,0:T(8,128)(2,1)S(1)}) fusion(f32[512,3072]{1,0:T(8,128)} %fusion.103, f32[3072]{0:T(1024)S(1)} %bitcast.214, bf16[3072,768]{1,0:T(8,128)(2,1)} %all-gather.12.cloned.1.call-done, bf16[1,512,768]{2,1,0:T(8,128)(2,1)S(1)} %copy-done.17, f32[512]{0:T(512)S(1)} %fusion.97), kind=kOutput, calls=%fused_computation.69 | convolution fusion | flops 2451698688 | bytes 14968832 | tf_op jit(solution)/shard_map/dot_general | solution.py:46
  263.0 9.0 %fusion.102 = f32[768,3072]{1,0:T(8,128)} fusion(bf16[512,3072]{1,0:T(8,128)(2,1)} %copy-done.39, f32[512,768]{1,0:T(8,128)} %copy-done.9, f32[768]{0:T(1024)S(1)} %convert_element_type.215, f32[768]{0:T(1024)S(1)} %convert_element_type.214, f32[512]{0:T(512)S(1)} %add_rsqrt_fusion, f32[512]{0:T(512)S(1)} %broadcast_multiply_fusion.4), kind=kOutput, calls=%fused_computation.150 | convolution fusion | flops 2417885184 | bytes 14166016 | tf_op jit(solution)/shard_map/dot_general | solution.py:40
  278.5 6.3 reduce.2
  287.2 4.2 all-to-all-start.2
  291.5 10.3 %fusion.101 = f32[3072,768]{1,0:T(8,128)} fusion(bf16[1,512,768]{2,1,0:T(8,128)(2,1)} %param.34, f32[512]{0:T(512)S(1)} %fusion.97, f32[512,3072]{1,0:T(8,128)} %fusion.103, f32[3072]{0:T(1024)S(1)} %bitcast.215), kind=kOutput, calls=%fused_computation.149 | convolution fusion | flops 2432827392 | bytes 16529408 | tf_op jit(solution)/shard_map/dot_general | solution.py:40
  302.0 9.0 %all-to-all-done.2 = bf16[4,2,49152]{2,1,0:T(2,128)(2,1)} async-done(((bf16[4,2,49152]{2,1,0:T(2,128)(2,1)}), bf16[4,2,49152]{2,1,0:T(2,128)(2,1)}, u32[]{:S(2)}, u32[]{:S(2)}) %all-to-all-start.2) | async-done | bytes 786464 | tf_op jit(solution)/shard_map/all_to_all | solution.py:267
  311.0 3.7 reshape.263
  317.3 108.2 %while.47 = (s32[]{:T(128)}, f32[2048,3,64]{0,2,1:T(8,128)S(1)}, f32[2048,3,64]{0,2,1:T(8,128)}, bf16[4,512,3,64]{1,3,2,0:T(8,128)(2,1)}, bf16[4,512,3,64]{1,3,2...) while((s32[]{:T(128)}, f32[2048,3,64]{0,2,1:T(8,128)S(1)}, ...), condition=%wide.region_12.13_spmd.clone, body=%wide.region_10.12_spmd.clone.sunk | while | flops 2062615040 | bytes 185846064 | solution.py:131
  320.9 4.9 multiply_reduce_fusion.7
  326.2 4.8 multiply_convert_fusion.2
  331.0 4.4 fusion.163
  335.4 6.4 fusion.164
  348.1 4.8 multiply_reduce_fusion.7
  352.9 4.9 multiply_convert_fusion.2
  357.8 4.5 fusion.163
  362.3 6.4 fusion.164
  375.0 4.8 multiply_reduce_fusion.7
  379.9 4.9 multiply_convert_fusion.2
  384.7 4.4 fusion.163
  389.1 6.4 fusion.164
  401.9 4.9 multiply_reduce_fusion.7
  407.0 4.8 multiply_convert_fusion.2
  411.9 4.4 fusion.163
  416.3 6.4 fusion.164
  431.9 4.8 copy.73
  436.7 97.4 %all_to_all.60 = bf16[1,2048,3,192]{3,2,0,1:T(4,128)(2,1)} all-to-all(bf16[1,2048,3,192]{3,2,0,1:T(4,128)(2,1)} %copy.73), channel_id=1, replica_groups=mesh['seq'=4,'shard'=8] {'seq'}, dimensions={1} | all-to-all | bytes 4718592 | tf_op jit(solution)/shard_map/all_to_all | solution.py:280
  534.1 7.2 %copy.77 = bf16[1,4,512,3,192]{2,1,4,3,0:T(4,128)(2,1)S(1)} copy(bf16[1,4,512,3,192]{4,3,2,1,0:T(4,128)(2,1)} %bitcast.196) | data formatting | bytes 4718592 | tf_op jit(solution)/shard_map/all_to_all | solution.py:280
  543.3 5.3 fusion.85
  556.7 58.7 %reduce-scatter.5.cloned.1.call-done = f32[96,2304]{1,0:T(8,128)} async-done(((f32[768,2304]{1,0:T(8,128)}), f32[96,2304]{1,0:T(8,128)}) %reduce-scatter.5.cloned.1.call-update) | async-done | bytes 884752 | tf_op jit(solution)/shard_map/reduce_scatter | solution.py:294
  617.5 9.1 %fusion.82 = bf16[1,512,768]{2,1,0:T(8,128)(2,1)} fusion(f32[512,768]{1,0:T(8,128)S(1)} %copy-done.11, bf16[3072,768]{1,0:T(8,128)(2,1)} %all-gather.12.cloned.1.call-done, f32[768]{0:T(1024)S(1)} %convert_element_type.219, f32[512,3072]{1,0:T(8,128)} %fusion.103, f32[3072]{0:T(1024)S(1)} %bitcast.216), kind=kOutput, calls=%fused_computation.113 | convolution fusion | flops 2432827392 | bytes 13384704 | tf_op jit(solution)/shard_map/dot_general | solution.py:236
  630.6 22.5 %all-reduce.17 = (bf16[768]{0:T(1024)(128)(2,1)S(1)}, bf16[768]{0:T(1024)(128)(2,1)S(1)}, bf16[768]{0:T(1024)(128)(2,1)S(1)}, bf16[768]{0:T(1024)(128)(2,1)S(1)}...) all-reduce(f32[768]{0:T(1024)S(1)} %get-tuple-element.268, ...), channel_id=2, replica_groups=mesh['seq'=4,'shard'=8] {'shard'}, use_global_device_ids=true, to_apply=%region_16.17.clone | all-reduce | flops 9216 | bytes 55296
  653.7 9.8 %all-reduce.19 = (bf16[96]{0:T(256)(128)(2,1)S(1)}, bf16[96]{0:T(256)(128)(2,1)S(1)}, bf16[96]{0:T(256)(128)(2,1)S(1)}, bf16[96]{0:T(256)(128)(2,1)S(1)}, bf16[9...) all-reduce(bf16[96]{0:T(256)(128)(2,1)S(1)} %dynamic-slice.44, ...), channel_id=1, replica_groups=mesh['seq'=4,'shard'=8] {'seq'}, use_global_device_ids=true, to_apply=%region_17.18 | all-reduce | flops 1152 | bytes 4608 | tf_op jit(solution)/shard_map/psum | solution.py:321
  671.1 24.8 %all-reduce.23.cloned.1.call-done = (bf16[96,2304]{1,0:T(8,128)(2,1)}, bf16[96,768]{1,0:T(8,128)(2,1)}, bf16[96,3072]{1,0:T(8,128)(2,1)}, bf16[384,768]{1,0:T(8,128)(2,1)}) async-done(((bf16[96,2304]{1,0:T(8,128)(2,1)}, bf16[96,768]{1,0:T(8,128)(2,1)}, bf16[96,3072]{1,0:T(8,128)(2,1)}, bf16[384,768]{1,0:T(8,128)(2,1)}), (bf16[96,2304]{1,0:T(8,128)(2,1)}, bf16[96,768]{1,0:T(8,128)(2,1)}, ...) | async-done | bytes 1769488 | tf_op jit(solution)/shard_map/psum | solution.py:323
  (282 shorter events, 153.1 us)
Async XLA Ops:
  7.2 35.0 %copy-start.4 = (bf16[1,512,768]{2,1,0:T(8,128)(2,1)S(1)}, bf16[1,512,768]{2,1,0:T(8,128)(2,1)}, u32[]{:S(2)}) copy-start(bf16[1,512,768]{2,1,0:T(8,128)(2,1)} %param.20) | copy-start | bytes 2359300
  7.2 39.4 %all-gather.6.cloned.1.call-start = ((), (), s32[]{:S(2)}) async-start(), calls=%async_computation.8 | async-start | bytes 3981312 | tf_op jit(solution)/shard_map/all_gather | solution.py:181
  7.9 225.8 %all-gather.8.cloned.1.call-start = ((), (), s32[]{:S(2)}) async-start(), calls=%async_computation.9 | async-start | bytes 1327104 | tf_op jit(solution)/shard_map/all_gather | solution.py:184
  8.7 229.0 %all-gather.10.cloned.1.call-start = ((), (), s32[]{:S(2)}) async-start(), calls=%async_computation.10 | async-start | bytes 5308416 | tf_op jit(solution)/shard_map/all_gather | solution.py:188
  40.8 5.8 copy-start.31
  40.8 5.8 copy-start.22
  42.2 4.4 copy-start.20
  42.6 4.0 copy-start.29
  58.7 74.5 %all-to-all-start = ((bf16[1,512,3,768]{1,2,0,3:T(4,128)(2,1)}), bf16[1,512,3,768]{1,2,0,3:T(4,128)(2,1)S(1)}, u32[]{:S(2)}, u32[]{:S(2)}) async-start(bf16[1,512,3,768]{1,2,0,3:T(4,128)(2,1)} %copy.62), calls=%async_computation | async-start | bytes 6291456 | tf_op jit(solution)/shard_map/all_to_all | solution.py:208
  63.0 183.0 %all-gather.12.cloned.1.call-start = ((), (), s32[]{:S(2)}) async-start(), calls=%async_computation.11 | async-start | bytes 5308416 | tf_op jit(solution)/shard_map/all_gather | solution.py:190
  180.3 4.8 copy-start.1
  198.3 6.6 copy-start.36
  200.7 23.1 %all-to-all-start.1 = ((bf16[4,2,49152]{2,1,0:T(2,128)(2,1)}), bf16[4,2,49152]{2,1,0:T(2,128)(2,1)S(1)}, u32[]{:S(2)}, u32[]{:S(2)}) async-start(bf16[4,2,49152]{2,1,0:T(2,128)(2,1)} %reshape.260), calls=%async_computation.1 | async-start | bytes 1572864 | tf_op jit(solution)/shard_map/all_to_all | solution.py:219
  204.2 346.4 %reduce-scatter.7.cloned.1.call-start = ((), (), s32[]{:S(2)}) async-start(), calls=%async_computation.13 | async-start | bytes 2654208 | tf_op jit(solution)/shard_map/reduce_scatter | solution.py:297
  215.5 76.0 %copy-start.26 = (f32[8,1,384]{2,1,0:T(1,128)}, f32[8,1,384]{2,1,0:T(1,128)S(1)}, u32[]{:S(2)}) copy-start(f32[8,1,384]{2,1,0:T(1,128)S(1)} %convert_element_type.263) | copy-start | bytes 36868
  226.4 7.4 %copy-start.5 = (bf16[1,512,768]{2,1,0:T(8,128)(2,1)S(1)}, bf16[1,512,768]{2,1,0:T(8,128)(2,1)}, u32[]{:S(2)}) copy-start(bf16[1,512,768]{2,1,0:T(8,128)(2,1)} %param.20) | copy-start | bytes 2359300
  237.7 8.3 %copy-start.17 = (bf16[1,512,768]{2,1,0:T(8,128)(2,1)S(1)}, bf16[1,512,768]{2,1,0:T(8,128)(2,1)}, u32[]{:S(2)}) copy-start(bf16[1,512,768]{2,1,0:T(8,128)(2,1)} %param.34) | copy-start | bytes 2359300
  246.0 9.5 %copy-start.10 = (f32[512,768]{1,0:T(8,128)S(1)}, f32[512,768]{1,0:T(8,128)}, u32[]{:S(2)}) copy-start(f32[512,768]{1,0:T(8,128)} %copy-done.9) | copy-start | bytes 4718596
  246.0 9.5 %copy-start.37 = (bf16[768,3072]{1,0:T(8,128)(2,1)S(1)}, bf16[768,3072]{1,0:T(8,128)(2,1)}, u32[]{:S(2)}) copy-start(bf16[768,3072]{1,0:T(8,128)(2,1)} %all-gather.10.cloned.1.call-done) | copy-start | bytes 14155780
  260.5 11.5 %copy-start.2 = (f32[512,768]{1,0:T(8,128)}, f32[512,768]{1,0:T(8,128)S(1)}, u32[]{:S(2)}) copy-start(f32[512,768]{1,0:T(8,128)S(1)} %get-tuple-element.341) | copy-start | bytes 4718596
  262.7 289.5 %reduce-scatter.9.cloned.1.call-start = ((), (), s32[]{:S(2)}) async-start(), calls=%async_computation.14 | async-start | bytes 10616832 | tf_op jit(solution)/shard_map/reduce_scatter | solution.py:301
  287.2 23.9 %all-to-all-start.2 = ((bf16[4,2,49152]{2,1,0:T(2,128)(2,1)}), bf16[4,2,49152]{2,1,0:T(2,128)(2,1)}, u32[]{:S(2)}, u32[]{:S(2)}) async-start(bf16[4,2,49152]{2,1,0:T(2,128)(2,1)} %reshape.262), calls=%async_computation.2 | async-start | bytes 1572864 | tf_op jit(solution)/shard_map/all_to_all | solution.py:267
  291.4 263.0 %reduce-scatter.11.cloned.1.call-start = ((), (), s32[]{:S(2)}) async-start(), calls=%async_computation.15 | async-start | bytes 10616832 | tf_op jit(solution)/shard_map/reduce_scatter | solution.py:303
  301.8 313.7 %reduce-scatter.5.cloned.1.call-start = ((), (), s32[]{:S(2)}) async-start(), calls=%async_computation.12 | async-start | bytes 7962624 | tf_op jit(solution)/shard_map/reduce_scatter | solution.py:294
  320.1 6.0 copy-start
  331.0 4.4 copy-start.14
  331.0 10.8 %slice-start = ((s8[6291456]{0:T(1024)(128)(4,1)}), s8[4194304]{0:T(1024)(128)(4,1)S(1)}, s32[]{:S(2)}) async-start(s8[6291456]{0:T(1024)(128)(4,1)} %bitcast.192), calls=%async_computation.17 | async-start | bytes 8388608 | tf_op jit(solution)/shard_map/while/body/eval_jaxpr/while
  335.4 6.4 slice-start.1
  347.3 5.6 copy-start
  357.8 4.5 copy-start.14
  357.8 11.0 %slice-start = ((s8[6291456]{0:T(1024)(128)(4,1)}), s8[4194304]{0:T(1024)(128)(4,1)S(1)}, s32[]{:S(2)}) async-start(s8[6291456]{0:T(1024)(128)(4,1)} %bitcast.192), calls=%async_computation.17 | async-start | bytes 8388608 | tf_op jit(solution)/shard_map/while/body/eval_jaxpr/while
  362.3 6.5 slice-start.1
  374.3 5.6 copy-start
  384.7 4.4 copy-start.14
  384.7 10.8 %slice-start = ((s8[6291456]{0:T(1024)(128)(4,1)}), s8[4194304]{0:T(1024)(128)(4,1)S(1)}, s32[]{:S(2)}) async-start(s8[6291456]{0:T(1024)(128)(4,1)} %bitcast.192), calls=%async_computation.17 | async-start | bytes 8388608 | tf_op jit(solution)/shard_map/while/body/eval_jaxpr/while
  389.1 6.4 slice-start.1
  401.1 5.9 copy-start
  411.9 4.4 copy-start.14
  411.9 10.8 %slice-start = ((s8[6291456]{0:T(1024)(128)(4,1)}), s8[4194304]{0:T(1024)(128)(4,1)S(1)}, s32[]{:S(2)}) async-start(s8[6291456]{0:T(1024)(128)(4,1)} %bitcast.192), calls=%async_computation.17 | async-start | bytes 8388608 | tf_op jit(solution)/shard_map/while/body/eval_jaxpr/while
  416.3 6.4 slice-start.1
  548.6 147.3 %all-reduce.23.cloned.1.call-start = ((), (), s32[]{:S(2)}) async-start(), calls=%async_computation.16 | async-start | bytes 3538944 | tf_op jit(solution)/shard_map/psum | solution.py:323
  554.4 63.0 %copy-start.11 = (f32[512,768]{1,0:T(8,128)S(1)}, f32[512,768]{1,0:T(8,128)}, u32[]{:S(2)}) copy-start(f32[512,768]{1,0:T(8,128)} %copy-done.9) | copy-start | bytes 4718596
  554.4 63.1 %copy-start.27 = (f32[8,1,384]{2,1,0:T(1,128)S(1)}, f32[8,1,384]{2,1,0:T(1,128)}, u32[]{:S(2)}) copy-start(f32[8,1,384]{2,1,0:T(1,128)} %copy-done.26) | copy-start | bytes 36868
  617.5 9.1 %copy-start.8 = (bf16[1,512,3,4,192]{1,4,3,2,0:T(8,128)(2,1)S(1)}, bf16[1,512,3,4,192]{1,4,3,2,0:T(8,128)(2,1)}, u32[]{:S(2)}) copy-start(bf16[1,512,3,4,192]{1,4,3,2,0:T(8,128)(2,1)} %copy-done.7) | copy-start | bytes 7077892
  617.5 9.4 %copy-start.38 = (bf16[768,2304]{1,0:T(8,128)(2,1)S(1)}, bf16[768,2304]{1,0:T(8,128)(2,1)}, u32[]{:S(2)}) copy-start(bf16[768,2304]{1,0:T(8,128)(2,1)} %all-gather.6.cloned.1.call-done) | copy-start | bytes 10616836
  626.9 3.7 copy-start.24
  627.0 41.3 %copy-start.3 = (f32[512,768]{1,0:T(8,128)S(1)}, f32[512,768]{1,0:T(8,128)}, u32[]{:S(2)}) copy-start(f32[512,768]{1,0:T(8,128)} %copy-done.2) | copy-start | bytes 4718596
  695.9 5.9 copy-start.19
  (21 other events, 53.3 us)
Sparse Core Ops, SparseCore 0:
  9.9 36.6 all-gather.5
  48.5 24.0 all-gather.7
  74.5 38.8 all-gather.9
  115.2 38.9 all-gather.11
  262.9 41.5 reduce-scatter.6
  308.2 76.4 reduce-scatter.8
  388.6 76.4 reduce-scatter.10
  548.7 66.6 reduce-scatter.4
  619.2 76.6 all-reduce.22
where the time goes:
time: 718 us; the launch traced here: 710 us
  matrix products  179 us (25%)
  waiting for transfers between devices  177 us (25%)
  blocking collectives  163 us (23%)
  other arithmetic  86.6 us (12%)
  local copies, waits for them, and re-layouts  73.4 us (10%)
  between operations  17.6 us (2%)
  starting transfers between devices  12.9 us (2%)
    all_to_all x1, blocking collectives, on_device(): lax.all_to_all(grad_packed, 'seq', split_axis=1, concat_axis=3, tiled=True)  97.4 us
    all_to_all x1, waiting for transfers between devices, on_device(): lax.all_to_all(projected.reshape(slots_here, local_len, 3, width), 'seq',...  69.6 us
    reduce_scatter x1, waiting for transfers between devices, on_device(): lax.psum_scatter(grad_w_qkv, 'shard', scatter_dimension=0, tiled=True)  58.7 us
    unnamed x2, blocking collectives  45.2 us
    dot_general x4, matrix products, contract_rows(): lax.dot_general(left, right, (((0,), (0,)), ((), ())), preferred_element_...  26.7 us
    unnamed x108, local copies, waits for them, and re-layouts  26.3 us
    dot_general x4, matrix products, one_block(): jnp.einsum('hqk,qhd->khd', weights.astype(jnp.bfloat16), grad_rows, prefe...  25.6 us
    psum x1, waiting for transfers between devices, on_device(): lax.psum(every_share[2].astype(jnp.bfloat16), 'seq').astype(jnp.float32)  24.8 us
  transfers between devices with their start and end apart: 12, of which 6 were waited for; matrix products, arithmetic and copies ran while one was open for 43% of the time, Pallas kernels for 0%

commit v1 on v0

v1 whole, which is shorter than its diff:
```python
import functools
import math

import jax
import jax.numpy as jnp
from jax import lax
from jax.experimental import pallas as pl
from jax.experimental.pallas import tpu as pltpu
from jax.sharding import PartitionSpec as P

HEAD_DIM = 64
EPS = 1e-05
GELU_C = 0.7978845608028654
GELU_K = 0.044715
MASKED = -1e30

BF = jnp.bfloat16
F32 = jnp.float32
MESH = pl.DeviceIdType.MESH
VMEM = pl.BlockSpec(memory_space=pltpu.VMEM)
ANY = pl.BlockSpec(memory_space=pl.ANY)

LN1G, LN1B, QB, VB, OB, LN2G, LN2B, FB, IB = range(9)
VECS = 12
VROWS = 16


def dot(left, right):
    return jnp.dot(left, right, preferred_element_type=F32)


def dot_t(left, right):
    return lax.dot_general(left, right, (((1,), (1,)), ((), ())), preferred_element_type=F32)


def mean_rows(values):
    return jnp.mean(values, -1, keepdims=True)


def unit_of(values):
    centred = values - mean_rows(values)
    inverse = lax.rsqrt(mean_rows(centred * centred) + EPS)
    return centred * inverse, inverse


def split3(values):
    high = values.astype(BF)
    rest = values - high.astype(F32)
    mid = rest.astype(BF)
    low = (rest - mid.astype(F32)).astype(BF)
    return high, mid, low


class Place:
    def __init__(self, shards):
        self.shards = shards
        per_plane = shards // 4
        q = lax.axis_index("seq")
        s = lax.axis_index("shard")
        self.q, self.s = q, s
        self.core = lax.rem(s, 2)
        plane, member = s // per_plane, lax.rem(s, per_plane)
        side = lax.rem(q + plane + member, 2)
        self.to = (plane, member * 4 + side * 2 + q // 2)
        group, side_here = s // 4, lax.rem(s // 2, 2)
        self.quarter = lax.rem(side_here + q + group, 2) + 2 * self.core
        self.origin = (self.quarter, q * per_plane + group)
        self.stays = (self.to[0] == q) & (self.to[1] == s)
        self.sibling = (q, s + 1 - 2 * self.core)
        self.beside = (q, s + 2 - 4 * side_here)
        self.quarters = [
            lax.rem(side_here + j // 2 + q + group, 2) + 2 * (j % 2) for j in range(4)
        ]


def relocation(n_seq, shards):
    per_plane = shards // 4
    pairs = []
    for q in range(n_seq):
        for s in range(shards):
            plane, member = s // per_plane, s % per_plane
            side = (q + plane + member) % 2
            pairs.append((q * shards + s, plane * shards + member * 4 + side * 2 + q // 2))
    return pairs


def remote(src, dst, send, recv, device):
    return pltpu.make_async_remote_copy(
        src_ref=src, dst_ref=dst, send_sem=send, recv_sem=recv, device_id=device, device_id_type=MESH
    )


def greet(here, devices, mover):
    barrier = pltpu.get_barrier_semaphore()
    for device in devices:
        pl.semaphore_signal(barrier, inc=1, device_id=device, device_id_type=MESH)

    @pl.when(jnp.logical_not(here.stays))
    def _():
        pl.semaphore_signal(barrier, inc=1, device_id=mover, device_id_type=MESH)
        pl.semaphore_wait(barrier, len(devices) + 1)

    @pl.when(here.stays)
    def _():
        pl.semaphore_wait(barrier, len(devices))


def forward_kernel(dims, *refs):
    shards, rows, width, heads, gather = dims
    n_in = 4
    tok, length_in, w_in, vec_in = refs[:n_in]
    (ka_o, va_o, kt_o, qat_o, ctxt_o, ctx_o, h1_o, wf_o, xown_o, len_o, vec_o, inb_o) = refs[
        n_in : n_in + 12
    ]
    (
        xs, wf, vg, lens, h1, ka, va, kt, vt, qat, ctxt, ctx,
        perm_s, perm_r, sib_s, sib_r, side_s, side_r, back_s, back_r,
        len_s, len_r, w_s, w_r, out_s, ctx_s, ctx_r,
    ) = refs[n_in + 12 :]
    here = Place(shards)
    core, s = here.core, here.s
    half = width // 2
    share = width // shards
    chunks = 4
    step = rows // chunks
    partner_y = (here.q, s + 4 - 8 * lax.rem(s // 4, 2))

    partners = [here.sibling, here.beside] + ([partner_y] if gather else [])
    greet(here, partners, here.origin)

    to_core = here.q // 2

    def block(ref, j, i):
        return ref.at[pl.ds(pl.multiple_of(j * rows + i * step, step), step), :]

    def perm_copy(i):
        return remote(
            tok.at[pl.ds(i * step, step), :], block(xs, to_core, i), perm_s.at[i], perm_r.at[i], here.to
        )

    def len_copy():
        return remote(length_in, lens, len_s, len_r, here.to)

    @pl.when(jnp.logical_not(here.stays))
    def _():
        for i in range(chunks):
            perm_copy(i).start()
        len_copy().start()

    @pl.when(here.stays)
    def _():
        for i in range(chunks):
            pltpu.make_async_copy(
                tok.at[pl.ds(i * step, step), :], block(xs, to_core, i), perm_r.at[i]
            ).start()
        pltpu.make_async_copy(length_in, lens, len_r).start()

    w_copies = []
    if gather:
        def columns(j, which):
            return pl.ds(pl.multiple_of(j * width + which * half, 128), half)

        mine = pl.ds(pl.multiple_of(s * share, share), share)
        for j in range(3):
            copy = remote(
                w_in.at[:, columns(j, 1 - core)], wf.at[mine, pl.ds(j * half, half)],
                w_s.at[j], w_r.at[j], here.sibling,
            )
            copy.start()
            w_copies.append(copy)
            copy = pltpu.make_async_copy(
                w_in.at[:, columns(j, core)], wf.at[mine, pl.ds(j * half, half)], w_s.at[4 + j]
            )
            copy.start()
            w_copies.append(copy)
        copy = remote(vec_in, vg.at[s], w_s.at[3], w_r.at[3], here.sibling)
        copy.start()
        w_copies.append(copy)
        copy = pltpu.make_async_copy(vec_in, vg.at[s], w_s.at[7])
        copy.start()
        w_copies.append(copy)
    else:
        copy = pltpu.make_async_copy(w_in, wf, w_s.at[0])
        copy.start()
        w_copies.append(copy)

    def hop(count, device, at):
        first = s // count * count
        rows_of = pl.ds(pl.multiple_of(first * share, share), count * share)
        one = remote(wf.at[rows_of, :], wf.at[rows_of, :], w_s.at[at], w_r.at[at], device)
        two = remote(
            vg.at[pl.ds(first, count)], vg.at[pl.ds(first, count)], w_s.at[at + 1], w_r.at[at + 1], device
        )
        one.start()
        two.start()
        return [one, two]

    def receive(i):
        pltpu.make_async_copy(tok.at[pl.ds(i * step, step), :], block(xs, core, i), perm_r.at[i]).wait()
        sib = remote(block(xs, core, i), block(xs, core, i), sib_s.at[i], sib_r.at[i], here.sibling)
        side = remote(block(xs, core, i), block(xs, 2 + core, i), side_s.at[i], side_r.at[i], here.beside)
        side.start()
        sib.start()
        return [sib, side]

    def relay(i):
        block_in = block(xs, 2 + core, i)
        remote(block_in, block_in, side_s.at[i], side_r.at[i], here.beside).wait_recv()
        copy = remote(block_in, block_in, back_s.at[i], back_r.at[i], here.sibling)
        copy.start()
        return copy

    moved = []
    hops = []
    if gather:
        for copy in w_copies:
            copy.wait()
        hops += hop(2, here.beside, 8)
    moved += receive(0)
    moved += receive(1)
    if gather:
        for copy in hops:
            copy.wait_recv()
        second = hop(4, partner_y, 10)
    moved += receive(2)
    moved += receive(3)

    def norm_one(first, count):
        def body(i, _):
            at = pl.ds(pl.multiple_of(first + i * 256, 256), 256)
            unit, _ = unit_of(xs[at, :].astype(F32))
            h1[at, :] = (unit * vec_o[LN1G : LN1G + 1, :] + vec_o[LN1B : LN1B + 1, :]).astype(BF)
            return 0

        lax.fori_loop(0, count // 256, body, 0)

    if gather:
        for copy in second:
            copy.wait_recv()
        for i in range(shards):
            piece = vg[i].astype(F32)
            vec_o[:, i * share : (i + 1) * share] = piece[:, :share]
            for r in range(4):
                at = (4 * i + r) * share
                inb_o[:, at : at + share] = jnp.broadcast_to(
                    piece[IB + r : IB + r + 1, :share], (8, share)
                )
    else:
        for copy in w_copies:
            copy.wait()
        vec_o[...] = vec_in[...].astype(F32)
        inb_o[...] = jnp.zeros_like(inb_o)

    pltpu.make_async_copy(length_in, lens, len_r).wait()
    length = lens[0:1, 0:1]
    lane = lax.broadcasted_iota(jnp.int32, (rows, 128), 1)
    row_at = lax.broadcasted_iota(jnp.int32, (rows, 128), 0)
    lower = lane < HEAD_DIM
    ones_rows = (lax.broadcasted_iota(jnp.int32, (16, rows), 0) == 0).astype(BF)
    q_rest = (lax.broadcasted_iota(jnp.int32, (64, 2 * rows), 0) == 3).astype(BF)
    for h in range(heads):
        qat[h, HEAD_DIM:, :] = q_rest

    def bias_half(at):
        full = vec_o[at : at + 1, :]
        return jnp.where(core == 0, full[:, :half], full[:, half:])

    def project(j):
        at = slice(j * rows, (j + 1) * rows)
        norm = h1[at, :]
        dead = jnp.where(here.quarters[j] * rows + row_at < length, 0.0, MASKED)
        k_rest = jnp.where(lane == HEAD_DIM + 3, dead, jnp.where(lane < HEAD_DIM + 3, 1.0, 0.0))
        v_rest = jnp.where(lane < HEAD_DIM + 3, -1.0, 0.0)
        if j < 2:
            q = (dot(norm, wf[:, :half]) + bias_half(QB)).astype(BF) * BF(HEAD_DIM**-0.5)
        k = dot(norm, wf[:, half : 2 * half])
        v = dot(norm, wf[:, 2 * half :]) + bias_half(VB)
        for i in range(heads // 2):
            two = slice(i * 128, (i + 1) * 128)
            kp, vp = k[:, two], v[:, two]
            ka[2 * i, at, :] = jnp.where(lower, kp, k_rest).astype(BF)
            ka[2 * i + 1, at, :] = jnp.where(lower, pltpu.roll(kp, 64, 1), k_rest).astype(BF)
            va[2 * i, at, :] = jnp.where(lower, vp, v_rest).astype(BF)
            va[2 * i + 1, at, :] = jnp.where(lower, pltpu.roll(vp, 64, 1), v_rest).astype(BF)
            turned = kp.astype(BF).T
            kt[2 * i, :, at] = turned[:64]
            kt[2 * i + 1, :, at] = turned[64:]
            turned = vp.astype(BF).T
            vt[2 * i, :64, at] = turned[:64]
            vt[2 * i + 1, :64, at] = turned[64:]
            vt[2 * i, 64:, at] = ones_rows
            vt[2 * i + 1, 64:, at] = ones_rows
            if j < 2:
                turned = q[:, two].T
                qat[2 * i, :64, at] = turned[:64]
                qat[2 * i + 1, :64, at] = turned[64:]

    for i in range(chunks):
        remote(block(xs, core, i), block(xs, 1 - core, i), sib_s.at[i], sib_r.at[i], here.sibling).wait_recv()
    norm_one(0, 2 * rows)
    project(0)
    project(1)
    relays = [relay(i) for i in range(chunks)]
    for i in range(chunks):
        pl_block = block(xs, 3 - core, i)
        remote(pl_block, pl_block, back_s.at[i], back_r.at[i], here.sibling).wait_recv()
    norm_one(2 * rows, 2 * rows)
    project(2)
    project(3)

    saves = []
    own = pl.ds(pl.multiple_of(core * rows, rows), rows)
    for at, (src, dst) in enumerate(
        ((ka, ka_o), (va, va_o), (kt, kt_o), (h1, h1_o), (wf, wf_o), (xs.at[own, :], xown_o), (lens, len_o))
    ):
        copy = pltpu.make_async_copy(src, dst, out_s.at[at])
        copy.start()
        saves.append(copy)

    size = 512
    keys = 4 * rows

    def attend(h, _):
        for qb in range(2 * rows // size):
            at = slice(qb * size, (qb + 1) * size)
            query = qat[h, :, at]

            def scores(c):
                return dot(ka[h, c * size : (c + 1) * size, :], query)

            ahead = scores(0)
            highest = total = None
            for c in range(keys // size):
                now = ahead
                if c + 1 < keys // size:
                    ahead = scores(c + 1)
                top = jnp.max(now, axis=0, keepdims=True)
                top = top if highest is None else jnp.maximum(highest, top)
                weights = jnp.exp(now - top).astype(BF)
                part = dot(vt[h, :, c * size : (c + 1) * size], weights)
                total = part if total is None else total * jnp.exp(highest - top) + part
                highest = top
            mass = total[64:65]
            result = (total[:64] / mass).astype(BF)
            ctxt[pl.ds(pl.multiple_of(h * 64, 64), 64), at] = result
            high, mid, low = split3(-(highest + jnp.log(mass)))
            index = lax.broadcasted_iota(jnp.int32, (16, size), 0)
            rest = jnp.where(index == 3, 1.0, 0.0)
            for r, term in enumerate((high, mid, low)):
                rest = jnp.where(index == r, term.astype(F32), rest)
            qat[h, 64:80, at] = rest.astype(BF)
        return 0

    lax.fori_loop(0, heads, attend, 0)

    mine = pl.ds(pl.multiple_of(core * half, 128), half)
    own = pl.ds(pl.multiple_of(core * rows, rows), rows)
    other = pl.ds(pl.multiple_of((1 - core) * rows, rows), rows)
    trade = remote(ctxt.at[:, other], ctx.at[mine, :], ctx_s, ctx_r, here.sibling)
    trade.start()
    local = pltpu.make_async_copy(ctxt.at[:, own], ctx.at[mine, :], out_s.at[7])
    local.start()
    for at, (src, dst) in enumerate(((qat, qat_o), (ctxt, ctxt_o))):
        copy = pltpu.make_async_copy(src, dst, out_s.at[8 + at])
        copy.start()
        saves.append(copy)
    local.wait()
    trade.wait()
    copy = pltpu.make_async_copy(ctx, ctx_o, out_s.at[10])
    copy.start()
    saves.append(copy)
    for copy in saves:
        copy.wait()

    @pl.when(jnp.logical_not(here.stays))
    def _():
        for i in range(chunks):
            perm_copy(i).wait_send()
        len_copy().wait_send()

    for copy in moved + relays:
        copy.wait_send()
    if gather:
        for copy in hops + second:
            copy.wait_send()


def attention_forward(dims, tok, length, w, vec):
    shards, rows, width, heads, gather = dims
    half = width // 2
    keys = 4 * rows
    out = [
        ((heads, keys, 128), BF),
        ((heads, keys, 128), BF),
        ((heads, 64, keys), BF),
        ((heads, 128, 2 * rows), BF),
        ((half, 2 * rows), BF),
        ((width, rows), BF),
        ((keys, width), BF),
        ((width, 3 * half), BF),
        ((rows, width), BF),
        ((8, 128), jnp.int32),
        ((VROWS, width), F32),
        ((8, 4 * width), F32),
    ]
    sems = pltpu.SemaphoreType.DMA
    return pl.pallas_call(
        functools.partial(forward_kernel, dims),
        out_shape=tuple(jax.ShapeDtypeStruct(*o) for o in out),
        in_specs=[ANY, VMEM, ANY, VMEM],
        out_specs=tuple([ANY] * 10 + [VMEM] * 2),
        scratch_shapes=[
            pltpu.VMEM((keys, width), BF),
            pltpu.VMEM((width, 3 * half), BF),
            pltpu.VMEM((shards, VROWS, 128), BF),
            pltpu.VMEM((8, 128), jnp.int32),
            pltpu.VMEM((keys, width), BF),
            pltpu.VMEM((heads, keys, 128), BF),
            pltpu.VMEM((heads, keys, 128), BF),
            pltpu.VMEM((heads, 64, keys), BF),
            pltpu.VMEM((heads, 80, keys), BF),
            pltpu.VMEM((heads, 128, 2 * rows), BF),
            pltpu.VMEM((half, 2 * rows), BF),
            pltpu.VMEM((width, rows), BF),
            sems((4,)), sems((4,)), sems((4,)), sems((4,)), sems((4,)), sems((4,)), sems((4,)), sems((4,)),
            sems, sems, sems((12,)), sems((12,)), sems((12,)), sems, sems,
        ],
        compiler_params=pltpu.CompilerParams(
            collective_id=0, has_side_effects=True, vmem_limit_bytes=56 * 2**20
        ),
        name="attention_forward",
    )(tok, length, w, vec)


def feed_kernel(dims, *refs):
    shards, rows, width, heads, _ = dims
    ctx, x, cot, lens, vec, inb, wo_h, wi_h, wf_h = refs[:9]
    out_o, ect_o, gmid_o, gwi_o, gwf_o, gwo_o, vec_o, gib_o = refs[9:17]
    wo, wi, wf, mid, h2, h2t, eo, eot, gh2, acc, in_s = refs[17:]
    here = Place(shards)
    loads = []
    for at, (src, dst) in enumerate(((wo_h, wo), (wi_h, wi), (wf_h, wf))):
        copy = pltpu.make_async_copy(src, dst, in_s.at[at])
        copy.start()
        loads.append(copy)

    def vector(at):
        return vec[at : at + 1, :]

    row_at = lax.broadcasted_iota(jnp.int32, (rows, 1), 0) + here.quarter * rows
    live = row_at < lens[0:1, 0:1]
    e_outer = jnp.where(live, cot[...].astype(F32), 0.0)
    eo[...] = e_outer.astype(BF)
    eot[...] = eo[...].T
    vec_o[...] = jnp.zeros_like(vec_o)
    vec_o[FB : FB + 1, :] = jnp.sum(e_outer, 0, keepdims=True)

    loads[0].wait()
    middle = x[...].astype(F32) + dot(ctx[...].T, wo[...]) + vector(OB)
    mid[...] = middle
    unit, _ = unit_of(middle)
    h2[...] = (unit * vector(LN2G) + vector(LN2B)).astype(BF)
    h2t[:width, :] = h2[...].T
    h2t[width:, :] = jnp.ones((16, rows), BF)
    acc[...] = middle + vector(FB)
    gh2[...] = jnp.zeros_like(gh2)
    loads[1].wait()
    loads[2].wait()

    size = 512

    def part(c, _):
        at = pl.ds(pl.multiple_of(c * size, size), size)
        wic, wfc = wi[:, at], wf[at, :]
        inner = dot(h2[...], wic) + inb[0:1, at]
        square = inner * inner
        swing = jnp.tanh(GELU_C * inner * (1.0 + GELU_K * square))
        active = (0.5 * inner * (1.0 + swing)).astype(BF)
        slope = 0.5 * (1.0 + swing) + 0.5 * inner * (1.0 - swing * swing) * (
            GELU_C * (1.0 + 3.0 * GELU_K * square)
        )
        e_inner = (dot_t(eo[...], wfc) * slope).astype(BF)
        acc[...] += dot(active, wfc)
        gh2[...] += dot_t(e_inner, wic)
        gwf_o[:, at] = dot(eot[...], active).astype(BF)
        grads = dot(h2t[...], e_inner)
        gwi_o[:, at] = grads[:width].astype(BF)
        gib_o[:, at] = grads[width : width + 8]
        return 0

    lax.fori_loop(0, 4 * width // size, part, 0)
    out_o[...] = acc[...].astype(BF)
    unit, inverse = unit_of(mid[...])
    e_norm = gh2[...]
    vec_o[LN2G : LN2G + 1, :] = jnp.sum(e_norm * unit, 0, keepdims=True)
    vec_o[LN2B : LN2B + 1, :] = jnp.sum(e_norm, 0, keepdims=True)
    e_unit = e_norm * vector(LN2G)
    grad_mid = jnp.where(live, cot[...].astype(F32), 0.0) + inverse * (
        e_unit - mean_rows(e_unit) - unit * mean_rows(e_unit * unit)
    )
    gmid_o[...] = grad_mid
    e_branch = grad_mid.astype(BF)
    vec_o[OB : OB + 1, :] = jnp.sum(e_branch.astype(F32), 0, keepdims=True)
    gwo_o[...] = dot(ctx[...], e_branch).astype(BF)
    ect_o[...] = dot_t(wo[...], e_branch).astype(BF)


def feed_forward(dims, ctx, x, cot, lens, vec, inb, wo, wi, wf):
    shards, rows, width, heads, _ = dims
    out = [
        ((rows, width), BF),
        ((width, rows), BF),
        ((rows, width), F32),
        ((width, 4 * width), BF),
        ((width, 4 * width), BF),
        ((width, width), BF),
        ((VROWS, width), F32),
        ((8, 4 * width), F32),
    ]
    return pl.pallas_call(
        functools.partial(feed_kernel, dims),
        out_shape=tuple(jax.ShapeDtypeStruct(*o) for o in out),
        in_specs=[VMEM] * 6 + [ANY] * 3,
        out_specs=tuple([VMEM] * 8),
        scratch_shapes=[
            pltpu.VMEM((width, width), BF),
            pltpu.VMEM((width, 4 * width), BF),
            pltpu.VMEM((4 * width, width), BF),
            pltpu.VMEM((rows, width), F32),
            pltpu.VMEM((rows, width), BF),
            pltpu.VMEM((width + 16, rows), BF),
            pltpu.VMEM((rows, width), BF),
            pltpu.VMEM((width, rows), BF),
            pltpu.VMEM((rows, width), F32),
            pltpu.VMEM((rows, width), F32),
            pltpu.SemaphoreType.DMA((3,)),
        ],
        compiler_params=pltpu.CompilerParams(vmem_limit_bytes=58 * 2**20),
        name="feed_forward",
    )(ctx, x, cot, lens, vec, inb, wo, wi, wf)


def backward_kernel(dims, *refs):
    shards, rows, width, heads, _ = dims
    ect, ka_h, va_h, kt_h, qat_h, ctxt_h, h1_h, wf_h, x, gmid, vec = refs[:11]
    gtok_o, gw_o, vec_o = refs[11:14]
    (
        ka, va, kt, qat, ctxt, h1, wf, dot_all, doat, grads, dk_sum, dv_sum, sib_out, sib_in, side_out, side_in,
        own_sum, gt, load_s, do_s, do_r, sib_s, sib_r, side_s, side_r, perm_s, perm_r,
    ) = refs[14:]
    here = Place(shards)
    core = here.core
    half = width // 2
    keys = 4 * rows
    chunks = 4
    step = rows // chunks

    loads = []
    for at, (src, dst) in enumerate(
        ((ctxt_h, ctxt), (qat_h, qat), (ka_h, ka), (va_h, va), (kt_h, kt), (wf_h, wf), (h1_h, h1))
    ):
        copy = pltpu.make_async_copy(src, dst, load_s.at[at])
        copy.start()
        loads.append(copy)

    greet(here, [here.sibling, here.beside], here.to)

    mine = pl.ds(pl.multiple_of(core * half, 128), half)
    theirs = pl.ds(pl.multiple_of((1 - core) * half, 128), half)
    own = pl.ds(pl.multiple_of(core * rows, rows), rows)
    trade = remote(ect.at[theirs, :], dot_all.at[:, own], do_s.at[0], do_r, here.sibling)
    trade.start()
    local = pltpu.make_async_copy(ect.at[mine, :], dot_all.at[:, own], do_s.at[1])
    local.start()
    local.wait()
    trade.wait()
    loads[0].wait()
    index = lax.broadcasted_iota(jnp.int32, (16, 2 * rows), 0)
    for h in range(heads):
        at = slice(h * 64, (h + 1) * 64)
        e_ctx = dot_all[at, :]
        delta = jnp.sum(e_ctx.astype(F32) * ctxt[at, :].astype(F32), 0, keepdims=True)
        doat[h, :64, :] = e_ctx
        rest = jnp.zeros((16, 2 * rows), F32)
        for r, term in enumerate(split3(delta)):
            rest = jnp.where(index == r, term.astype(F32), rest)
        doat[h, 64:80, :] = rest.astype(BF)
        doat[h, 80:, :] = jnp.zeros((48, 2 * rows), BF)
    for copy in loads[1:]:
        copy.wait()

    size = 512
    parts = 2 * rows // size

    def attend(h, _):
        head = pl.ds(pl.multiple_of(h * 64, 64), 64)
        for qb in range(parts):
            at = slice(qb * size, (qb + 1) * size)
            query, e_ctx = qat[h, :, at], doat[h, :, at]
            e_query = None
            for c in range(keys // size):
                to = slice(c * size, (c + 1) * size)
                weights = jnp.exp(dot(ka[h, to, :], query))
                e_scores = (weights * dot(va[h, to, :], e_ctx)).astype(BF)
                weights = weights.astype(BF)
                e_value = dot_t(e_ctx[:64], weights)
                e_key = dot_t(query[:64], e_scores)
                part = dot(kt[h, :, to], e_scores)
                e_query = part if e_query is None else e_query + part
                if qb > 0:
                    e_value += dv_sum[:, to]
                    e_key += dk_sum[:, to]
                if qb < parts - 1:
                    dv_sum[:, to] = e_value
                    dk_sum[:, to] = e_key
                else:
                    grads[pl.ds(pl.multiple_of(half + h * 64, 64), 64), to] = e_key.astype(BF)
                    grads[pl.ds(pl.multiple_of(2 * half + h * 64, 64), 64), to] = e_value.astype(BF)
            grads[head, at] = (e_query * HEAD_DIM**-0.5).astype(BF)
        return 0

    lax.fori_loop(0, heads, attend, 0)

    def partial_of(j, own_chip):
        at = pl.ds(pl.multiple_of(j * rows, rows), rows)
        if own_chip:
            return dot(wf[...], grads[:, at])
        return dot(wf[:, half:], grads[half:, at])

    sib_out[0] = partial_of(3 - core, False).astype(BF)
    away = remote(sib_out.at[0], sib_in.at[0], sib_s.at[0], sib_r.at[0], here.sibling)
    away.start()
    beside = partial_of(2 + core, False)
    away.wait_recv()
    side_out[...] = (beside + sib_in[0].astype(F32)).astype(BF)
    sides = []
    for i in range(chunks):
        at = slice(i * step, (i + 1) * step)
        copy = remote(side_out.at[:, at], side_in.at[:, at], side_s.at[i], side_r.at[i], here.beside)
        copy.start()
        sides.append(copy)
    sib_out[1] = partial_of(1 - core, True).astype(BF)
    near = remote(sib_out.at[1], sib_in.at[1], sib_s.at[1], sib_r.at[1], here.sibling)
    near.start()
    own_part = partial_of(core, True)
    near.wait_recv()
    own_sum[...] = own_part + sib_in[1].astype(F32)

    gw_o[:, :half] = dot(grads[:half, : 2 * rows], h1[: 2 * rows, :]).T.astype(BF)
    gw_o[:, half : 2 * half] = dot(grads[half : 2 * half, :], h1[...]).T.astype(BF)
    gw_o[:, 2 * half :] = dot(grads[2 * half :, :], h1[...]).T.astype(BF)
    vec_o[...] = jnp.zeros_like(vec_o)

    def row_sums(values):
        wide = values.shape[1]
        folded = values[:, :128].astype(F32)
        for i in range(1, wide // 128):
            folded += values[:, i * 128 : (i + 1) * 128].astype(F32)
        return jnp.sum(folded.T, 0, keepdims=True)

    vec_o[QB : QB + 1, :half] = row_sums(grads[:half, : 2 * rows])
    vec_o[VB : VB + 1, :half] = row_sums(grads[2 * half :, :])

    gain = vec[LN1G : LN1G + 1, :]

    def perm_copy(i):
        at = pl.ds(i * step, step)
        return remote(gt.at[at, :], gtok_o.at[at, :], perm_s.at[i], perm_r.at[i], here.origin)

    def stay_copy(i):
        at = pl.ds(i * step, step)
        return pltpu.make_async_copy(gt.at[at, :], gtok_o.at[at, :], perm_r.at[i])

    gain_sum = shift_sum = None
    for i in range(chunks):
        at = slice(i * step, (i + 1) * step)
        sides[i].wait_recv()
        e_norm = (own_sum[:, at] + side_in[:, at].astype(F32)).T
        unit, inverse = unit_of(x[at, :].astype(F32))
        e_unit = e_norm * gain
        result = gmid[at, :] + inverse * (
            e_unit - mean_rows(e_unit) - unit * mean_rows(e_unit * unit)
        )
        gt[at, :] = result.astype(BF)

        @pl.when(jnp.logical_not(here.stays))
        def _():
            perm_copy(i).start()

        @pl.when(here.stays)
        def _():
            stay_copy(i).start()

        gains = jnp.sum(e_norm * unit, 0, keepdims=True)
        shifts = jnp.sum(e_norm, 0, keepdims=True)
        gain_sum = gains if i == 0 else gain_sum + gains
        shift_sum = shifts if i == 0 else shift_sum + shifts
    vec_o[LN1G : LN1G + 1, :] = gain_sum
    vec_o[LN1B : LN1B + 1, :] = shift_sum

    for copy in [away, near] + sides:
        copy.wait_send()
    for i in range(chunks):
        stay_copy(i).wait()

    @pl.when(jnp.logical_not(here.stays))
    def _():
        for i in range(chunks):
            perm_copy(i).wait_send()


def attention_backward(dims, *args):
    shards, rows, width, heads, _ = dims
    half = width // 2
    keys = 4 * rows
    out = [((rows, width), BF), ((width, 3 * half), BF), ((VROWS, width), F32)]
    sems = pltpu.SemaphoreType.DMA
    return pl.pallas_call(
        functools.partial(backward_kernel, dims),
        out_shape=tuple(jax.ShapeDtypeStruct(*o) for o in out),
        in_specs=[VMEM] + [ANY] * 7 + [VMEM] * 3,
        out_specs=(ANY, VMEM, VMEM),
        scratch_shapes=[
            pltpu.VMEM((heads, keys, 128), BF),
            pltpu.VMEM((heads, keys, 128), BF),
            pltpu.VMEM((heads, 64, keys), BF),
            pltpu.VMEM((heads, 128, 2 * rows), BF),
            pltpu.VMEM((half, 2 * rows), BF),
            pltpu.VMEM((keys, width), BF),
            pltpu.VMEM((width, 3 * half), BF),
            pltpu.VMEM((half, 2 * rows), BF),
            pltpu.VMEM((heads, 128, 2 * rows), BF),
            pltpu.VMEM((3 * half, keys), BF),
            pltpu.VMEM((64, keys), F32),
            pltpu.VMEM((64, keys), F32),
            pltpu.VMEM((2, width, rows), BF),
            pltpu.VMEM((2, width, rows), BF),
            pltpu.VMEM((width, rows), BF),
            pltpu.VMEM((width, rows), BF),
            pltpu.VMEM((width, rows), F32),
            pltpu.VMEM((rows, width), BF),
            sems((7,)), sems((2,)), sems, sems((2,)), sems((2,)), sems((4,)), sems((4,)), sems((4,)), sems((4,)),
        ],
        compiler_params=pltpu.CompilerParams(
            collective_id=1, has_side_effects=True, vmem_limit_bytes=58 * 2**20
        ),
        name="attention_backward",
    )(*args)


def on_device(
    tokens, ln1_gain, ln1_shift, w_qkv, q_bias, v_bias, w_out, out_bias, ln2_gain, ln2_shift, w_in, in_bias,
    w_fin, fin_bias, cotangent, lengths, n_seq, shards,
):
    _, rows, width = tokens.shape
    heads = width // HEAD_DIM // 2
    half = width // 2
    share = width // shards
    gather = shards == 8
    dims = (shards, rows, width, heads, gather)
    axes = ("seq", "shard")
    there = relocation(n_seq, shards)
    back = [(b, a) for a, b in there]
    core = lax.rem(lax.axis_index("shard"), 2)

    packed = jnp.concatenate(
        [v.reshape(-1, share) for v in (ln1_gain, ln1_shift, q_bias, v_bias, out_bias, ln2_gain, ln2_shift, fin_bias, in_bias)]
    )
    length = jnp.broadcast_to(lengths.reshape(1, 1), (8, 128))
    if gather:
        vec = jnp.pad(packed, ((0, VROWS - VECS), (0, 128 - share)))
        w_here = w_qkv
    else:
        every = lax.all_gather(packed, "shard", axis=1, tiled=True)
        vec = jnp.pad(every, ((0, VROWS - VECS), (0, 0)))
        full_w = lax.all_gather(w_qkv, "shard", axis=0, tiled=True)
        w_here = lax.dynamic_index_in_dim(
            full_w.reshape(width, 3, 2, half), core, 2, keepdims=False
        ).reshape(width, 3 * half)
    (ka, va, kt, qat, ctxt, ctx, h1, wf, x, lens, vecs, inb) = attention_forward(
        dims, tokens.reshape(rows, width), length, w_here, vec
    )
    if not gather:
        inb = jnp.broadcast_to(
            lax.all_gather(in_bias, "shard", axis=0, tiled=True).astype(F32)[None], (8, 4 * width)
        )
    full_wo = lax.all_gather(w_out, "shard", axis=0, tiled=True)
    full_wi = lax.all_gather(w_in, "shard", axis=0, tiled=True)
    full_wf = lax.all_gather(w_fin, "shard", axis=0, tiled=True)
    cot = lax.ppermute(cotangent.reshape(rows, width), axes, there)
    out, ect, gmid, gwi, gwf, gwo, vec_two, gib = feed_forward(
        dims, ctx, x, cot, lens, vecs, inb, full_wo, full_wi, full_wf
    )
    output = lax.ppermute(out, axes, back).reshape(tokens.shape)
    gtok, gw, vec_one = attention_backward(
        dims, ect, ka, va, kt, qat, ctxt, h1, wf, x, gmid, vecs
    )

    def total(grad, dim):
        part = lax.psum_scatter(grad, "shard", scatter_dimension=dim, tiled=True)
        return lax.psum(part, "seq").astype(F32)

    total_wi = total(gwi, 0)
    total_wf = total(gwf, 1).T
    total_wo = total(gwo, 0)
    wide = jnp.zeros((width, 3, 2, half), BF)
    wide = lax.dynamic_update_index_in_dim(wide, gw.reshape(width, 3, half), core, 2)
    total_w = total(wide.reshape(width, 3 * width), 0)

    halves = jnp.zeros((2, 2, half), F32)
    halves = lax.dynamic_update_index_in_dim(halves, vec_one[QB : VB + 1, :half], core, 1).reshape(2, width)
    sums = jnp.concatenate(
        (vec_one[:QB], halves, vec_two[OB:IB], gib[0].reshape(4, width))
    )
    sums = lax.psum(sums, axes)
    s = lax.axis_index("shard")
    mine = lax.dynamic_slice_in_dim(sums[:IB], s * share, share, 1)
    total_ib = lax.dynamic_slice_in_dim(sums[IB:].reshape(-1), s * 4 * share, 4 * share, 0)
    return (
        output,
        gtok.reshape(tokens.shape),
        mine[LN1G],
        mine[LN1B],
        total_w,
        mine[QB],
        mine[VB],
        total_wo,
        mine[OB],
        mine[LN2G],
        mine[LN2B],
        total_wi,
        total_ib,
        total_wf,
        mine[FB],
    )


def solution(mesh):
    vector, matrix, rows = P("shard"), P("shard", None), P("shard", "seq", None)
    return jax.shard_map(
        functools.partial(on_device, n_seq=mesh.shape["seq"], shards=mesh.shape["shard"]),
        mesh=mesh,
        in_specs=(
            rows, vector, vector, matrix, vector, vector, matrix, vector, vector, vector, matrix, vector,
            matrix, vector, rows, vector,
        ),
        out_specs=(
            rows, rows, vector, vector, matrix, vector, vector, matrix, vector, vector, vector, matrix,
            vector, matrix, vector,
        ),
        check_vma=False,
    )
```

time: 718 us -> 604 us (0.84)
  Pallas kernels: 0 us -> 268 us
  matrix products: 179 us -> 0 us
  blocking collectives: 163 us -> 65.8 us
  other arithmetic: 86.6 us -> 4.01 us
  waiting for transfers between devices: 177 us -> 143 us
  local copies, waits for them, and re-layouts: 73.4 us -> 91.6 us
    pallas_call x0 -> x3, Pallas kernels: none -> 268 us  [the longest x1 142 us: attention_forward(): pl.pallas_call(functools.partial(forward_kernel, dims), out_shape=tuple((...]
    dot_general x40 -> x0, matrix products: 179 us -> none  [the longest x4 26.7 us: contract_rows(): lax.dot_general(left, right, (((0,), (0,)), ((), ())), preferred_element_...]
    all_to_all x1 -> x0, blocking collectives: 97.4 us -> none  [on_device(): lax.all_to_all(grad_packed, 'seq', split_axis=1, concat_axis=3, tiled=True)]
    all_to_all x3 -> x0, waiting for transfers between devices: 87 us -> none  [the longest x1 69.6 us: on_device(): lax.all_to_all(projected.reshape(slots_here, local_len, 3, width), 'seq',...]
    psum x1, blocking collectives: 9.81 us -> 65.8 us  [on_device(): sums = lax.psum(sums, axes)]
    dynamic_update_slice x4 -> x2, local copies, waits for them, and re-layouts: 2.78 us -> 54.5 us  [the longest x1 54.5 us: on_device(): lax.dynamic_update_index_in_dim(wide, gw.reshape(width, 3, half), core, 2)]
    unnamed x2 -> x0, blocking collectives: 45.2 us -> none
    reduce_scatter x4 -> x3, waiting for transfers between devices: 58.7 us -> 102 us  [total(): part = lax.psum_scatter(grad, 'shard', scatter_dimension=dim, tiled=True)]
  transfers between devices with their start and end apart: 12 -> 10, of which waited for: 6 -> 4; matrix products, arithmetic and copies ran while one was open for 43% -> 14% of each run, Pallas kernels for 0% -> 40%
where the time goes in v1:
time: 604 us; the launch traced here: 598 us
  Pallas kernels  268 us (44%)
  waiting for transfers between devices  143 us (24%)
  local copies, waits for them, and re-layouts  91.6 us (15%)
  blocking collectives  65.8 us (11%)
  between operations  15 us (2%)
  starting transfers between devices  10.4 us (2%)
    pallas_call x1, Pallas kernels, attention_forward(): pl.pallas_call(functools.partial(forward_kernel, dims), out_shape=tuple((...  142 us
    reduce_scatter x3, waiting for transfers between devices, total(): part = lax.psum_scatter(grad, 'shard', scatter_dimension=dim, tiled=True)  102 us
    pallas_call x1, Pallas kernels, attention_backward(): pl.pallas_call(functools.partial(backward_kernel, dims), out_shape=tuple(...  97.9 us
    psum x1, blocking collectives, on_device(): sums = lax.psum(sums, axes)  65.8 us
    dynamic_update_slice x1, local copies, waits for them, and re-layouts, on_device(): lax.dynamic_update_index_in_dim(wide, gw.reshape(width, 3, half), core, 2)  54.5 us
    pallas_call x1, Pallas kernels, feed_forward(): pl.pallas_call(functools.partial(feed_kernel, dims), out_shape=tuple((jax...  28.6 us
    all_gather x1, waiting for transfers between devices, on_device(): full_wf = lax.all_gather(w_fin, 'shard', axis=0, tiled=True)  19.8 us
    psum x1, waiting for transfers between devices, total(): return lax.psum(part, 'seq').astype(F32)  18 us
  transfers between devices with their start and end apart: 10, of which 4 were waited for; matrix products, arithmetic and copies ran while one was open for 14% of the time, Pallas kernels for 40%

profile of v1, /device:TPU:1, one launch (start us, length us, event | category | flops | bytes accessed | tf_op | source)
XLA Modules:
  0.0 598.1 jit_solution(13709888802434359311)
XLA Ops:
  7.2 0.0 all-gather.4.cloned.1.call-start
  7.2 0.7 all-gather.4.cloned.1.call-update
  7.9 0.0 all-gather.6.cloned.1.call-start
  8.0 0.7 all-gather.6.cloned.1.call-update
  8.7 0.0 all-gather.8.cloned.1.call-start
  8.7 0.7 all-gather.8.cloned.1.call-update
  9.4 0.0 reduce-scatter.13.cloned.1.call-start
  9.4 5.5 collective-permute-start
  14.9 0.8 reshape.91
  16.3 0.8 concatenate.6
  17.2 0.6 pad.4.refs_3_
  17.8 0.6 broadcast_in_dim.22.refs_1_
  18.4 141.9 %attention_forward.1 = (bf16[6,2048,128]{2,1,0:T(8,128)(2,1)}, bf16[6,2048,128]{2,1,0:T(8,128)(2,1)}, bf16[6,64,2048]{2,1,0:T(8,128)(2,1)}, bf16[6,128,1024]{2,1...) custom-call(bf16[512,768]{1,0:T(8,128)(2,1)} %bitcast.41, ...), custom_call_target="tpu_custom_call" | custom-call | tf_op jit(solution)/shard_map/attention_forward/pallas_call | solution.py:407
  160.3 0.0 all-gather.4.cloned.1.call-done.refs_6_
  160.3 19.8 %all-gather.8.cloned.1.call-done.refs_8_ = bf16[3072,768]{1,0:T(8,128)(2,1)} async-done(((bf16[384,768]{1,0:T(8,128)(2,1)}), bf16[3072,768]{1,0:T(8,128)(2,1)}) %all-gather.8.cloned.1.call-update) | async-done | bytes 4718608 | tf_op jit(solution)/shard_map/all_gather | solution.py:789
  180.1 28.6 %feed_forward.1 = (bf16[512,768]{1,0:T(8,128)(2,1)}, bf16[768,512]{1,0:T(8,128)(2,1)}, f32[512,768]{1,0:T(8,128)}, bf16[768,3072]{1,0:T(8,128)(2,1)}, bf16[768,3...) custom-call(bf16[768,512]{1,0:T(8,128)(2,1)} %get-tuple-element.38.refs_0_, ...), custom_call_target="tpu_custom_call" | custom-call | tf_op jit(solution)/shard_map/feed_forward/pallas_call | solution.py:520
  208.7 6.7 %copy.42 = bf16[768,3072]{0,1:T(8,128)(2,1)} copy(bf16[768,3072]{1,0:T(8,128)(2,1)} %get-tuple-element.60) | data formatting | bytes 9437184
  215.5 0.0 reduce-scatter.9.cloned.1.call-start
  215.5 0.5 reduce-scatter.9.cloned.1.call-update
  216.1 0.0 reduce-scatter.7.cloned.1.call-start
  216.1 97.9 %attention_backward.1 = (bf16[512,768]{1,0:T(8,128)(2,1)}, bf16[768,1152]{1,0:T(8,128)(2,1)}, f32[16,768]{1,0:T(8,128)}) custom-call(bf16[768,512]{1,0:T(8,128)(2,1)} %get-tuple-element.44.refs_0_, bf16[6,2048,128]{2,1,0:T(8,128)(2,1)} %get-tuple-element.45.refs_1_, bf16[6,2048,128]{2,1,0:T(8,128)(2,1)} %get-tuple-element.46.refs_2_, ...), custom_call_target="tpu_custom_call" | custom-call | tf_op jit(solution)/shard_map/attention_backward/pallas_call | solution.py:718
  314.1 2.6 copy.39
  316.7 8.4 %copy.40 = bf16[768,3,1,384]{3,2,1,0:T(2,128)(2,1)} copy(bf16[768,3,1,384]{0,3,1,2:T(8,128)(2,1)S(1)} %bitcast.39) | data formatting | bytes 3538944 | tf_op jit(solution)/shard_map/jit(dynamic_update_index_in_dim)/broadcast_in_dim | solution.py:807
  325.1 1.8 broadcast_in_dim.25
  327.0 54.5 %dynamic_update_slice.9 = bf16[768,3,2,384]{3,2,1,0:T(2,128)(2,1)S(1)} dynamic-update-slice(bf16[768,3,2,384]{3,2,1,0:T(2,128)(2,1)S(1)} %broadcast_in_dim.25, bf16[768,3,1,384]{3,2,1,0:T(2,128)(2,1)} %copy.40, s32[]{:T(128)} %constant.9.clone.1, s32[]{:T(128)} %constant.9.clone.1, s32[]{:T(128)S(6)} %select_n.12, s32[]{:T(128)} %constant.9.clone.1) | dynamic-update-slice | bytes 3538948 | tf_op jit(solution)/shard_map/jit(dynamic_update_index_in_dim)/dynamic_update_slice | solution.py:807
  381.4 4.0 reshape.96
  385.5 0.0 reduce-scatter.11.cloned.1.call-start
  385.5 0.7 reduce-scatter.11.cloned.1.call-update
  386.2 0.0 all-reduce.4.cloned.1.call-start
  386.3 2.1 copy.43
  388.4 44.4 %reduce-scatter.7.cloned.1.call-done = bf16[96,2304]{1,0:T(8,128)(2,1)} async-done(((bf16[768,2304]{1,0:T(8,128)(2,1)}), bf16[96,2304]{1,0:T(8,128)(2,1)}) %reduce-scatter.7.cloned.1.call-update) | async-done | bytes 442384 | tf_op jit(solution)/shard_map/reduce_scatter | solution.py:800
  432.8 57.3 %reduce-scatter.11.cloned.1.call-done = bf16[96,3072]{1,0:T(8,128)(2,1)} async-done(((bf16[768,3072]{1,0:T(8,128)(2,1)}), bf16[96,3072]{1,0:T(8,128)(2,1)}) %reduce-scatter.11.cloned.1.call-update) | async-done | bytes 589840 | tf_op jit(solution)/shard_map/reduce_scatter | solution.py:800
  490.1 0.7 slice.42
  490.9 4.6 collective-permute-start.1
  495.5 0.7 slice_bitcast_fusion
  496.3 0.9 slice_reduce_fusion
  497.2 0.7 slice.44
  498.0 65.8 %psum.35 = f32[12,768]{1,0:T(8,128)S(1)} all-reduce(f32[12,768]{1,0:T(8,128)S(1)} %pad_maximum_fusion), channel_id=1, replica_groups=mesh['seq'=4,'shard'=8] {'seq','shard'}, use_global_device_ids=true, to_apply=%region_0.1 | all-reduce | flops 9216 | bytes 73728 | tf_op jit(solution)/shard_map/psum | solution.py:815
  563.9 0.7 dynamic_slice.7
  564.5 0.1 constant_dynamic-slice_fusion
  564.6 0.5 slice_bitcast_fusion.1
  565.1 18.0 %all-reduce.4.cloned.1.call-done = (bf16[384,768]{0,1:T(8,128)(2,1)}, bf16[96,2304]{1,0:T(8,128)(2,1)}, bf16[96,768]{1,0:T(8,128)(2,1)}, bf16[96,3072]{1,0:T(8,128)(2,1)}) async-done(((bf16[384,768]{0,1:T(8,128)(2,1)}, bf16[96,2304]{1,0:T(8,128)(2,1)}, bf16[96,768]{1,0:T(8,128)(2,1)}, bf16[96,3072]{1,0:T(8,128)(2,1)}), (bf16[384,768]{0,1:T(8,128)(2,1)}, bf16[96,2304]{1,0:T(8,128)(2,1)}, ...) | async-done | bytes 1769488 | tf_op jit(solution)/shard_map/psum | solution.py:801
  583.1 2.3 convert_element_type.14
  585.4 2.3 copy.41
  587.7 1.0 convert_element_type.12
  588.7 0.7 convert_element_type.13
  589.5 0.9 copy.54
  590.3 0.9 copy.55
  (27 shorter events, 0.2 us)
Async XLA Ops:
  7.2 153.1 %all-gather.4.cloned.1.call-start = ((), (), s32[]{:S(2)}) async-start(), calls=%async_computation.4 | async-start | bytes 1327104 | tf_op jit(solution)/shard_map/all_gather | solution.py:787
  7.9 152.4 %all-gather.6.cloned.1.call-start = ((), (), s32[]{:S(2)}) async-start(), calls=%async_computation.5 | async-start | bytes 5308416 | tf_op jit(solution)/shard_map/all_gather | solution.py:788
  8.7 171.5 %all-gather.8.cloned.1.call-start = ((), (), s32[]{:S(2)}) async-start(), calls=%async_computation.6 | async-start | bytes 5308416 | tf_op jit(solution)/shard_map/all_gather | solution.py:789
  9.4 376.9 %reduce-scatter.13.cloned.1.call-start = ((), (), s32[]{:S(2)}) async-start(), calls=%async_computation.10 | async-start | bytes 5308416
  9.4 150.8 %collective-permute-start = (bf16[512,768]{1,0:T(8,128)(2,1)}, bf16[512,768]{1,0:T(8,128)(2,1)S(1)}, u32[]{:S(2)}, u32[]{:S(2)}) collective-permute-start(bf16[512,768]{1,0:T(8,128)(2,1)} %bitcast.55), channel_id=1, source_target_pairs={{0,0},{1,6},{2,10},{3,12},{4,16},{5,22},{6,26},{7,28},{8,2},{9,4},... | collective-permute-start | bytes 2359304 | tf_op jit(solution)/shard_map/ppermute | solution.py:790
  160.2 19.9 %copy-start = (bf16[512,768]{1,0:T(8,128)(2,1)}, bf16[512,768]{1,0:T(8,128)(2,1)S(1)}, u32[]{:S(2)}) copy-start(bf16[512,768]{1,0:T(8,128)(2,1)S(1)} %collective-permute-done.refs_2_) | copy-start | bytes 2359300
  215.5 172.9 %reduce-scatter.9.cloned.1.call-start = ((), (), s32[]{:S(2)}) async-start(), calls=%async_computation.8 | async-start | bytes 1327104 | tf_op jit(solution)/shard_map/reduce_scatter | solution.py:800
  216.1 216.7 %reduce-scatter.7.cloned.1.call-start = ((), (), s32[]{:S(2)}) async-start(), calls=%async_computation.7 | async-start | bytes 3981312 | tf_op jit(solution)/shard_map/reduce_scatter | solution.py:800
  385.5 104.7 %reduce-scatter.11.cloned.1.call-start = ((), (), s32[]{:S(2)}) async-start(), calls=%async_computation.9 | async-start | bytes 5308416 | tf_op jit(solution)/shard_map/reduce_scatter | solution.py:800
  385.5 105.4 %copy-start.4 = (bf16[512,768]{1,0:T(8,128)(2,1)S(1)}, bf16[512,768]{1,0:T(8,128)(2,1)}, u32[]{:S(2)}) copy-start(bf16[512,768]{1,0:T(8,128)(2,1)} %get-tuple-element.43) | copy-start | bytes 2359300
  386.2 196.9 %all-reduce.4.cloned.1.call-start = ((), (), s32[]{:S(2)}) async-start(), calls=%async_computation.11 | async-start | bytes 3538944 | tf_op jit(solution)/shard_map/psum | solution.py:801
  490.9 74.2 %collective-permute-start.1 = (bf16[512,768]{1,0:T(8,128)(2,1)S(1)}, bf16[512,768]{1,0:T(8,128)(2,1)S(1)}, u32[]{:S(2)}, u32[]{:S(2)}) collective-permute-start(bf16[512,768]{1,0:T(8,128)(2,1)S(1)} %copy-done.4), channel_id=1, source_target_pairs={{0,0},{6,1},{10,2},{12,3},{16,4},{22,5},{26,6},{28,7},{2,8},{4,9},... | collective-permute-start | bytes 2359304 | tf_op jit(solution)/shard_map/ppermute | solution.py:794
  583.1 4.6 copy-start.2
  583.1 5.6 copy-start.3
  583.1 7.2 %copy-start.1 = (bf16[512,768]{1,0:T(8,128)(2,1)S(1)}, bf16[512,768]{1,0:T(8,128)(2,1)}, u32[]{:S(2)}) copy-start(bf16[512,768]{1,0:T(8,128)(2,1)} %get-tuple-element.53) | copy-start | bytes 2359300
Sparse Core Ops, SparseCore 0:
  9.9 64.8 all-gather.3
  76.6 59.7 all-gather.5
  138.3 41.7 all-gather.7
  215.6 57.5 reduce-scatter.12
  277.2 42.8 reduce-scatter.8
  385.6 47.1 reduce-scatter.6
  436.2 53.8 reduce-scatter.10
  493.5 89.5 all-reduce.3

commit v2 on v1

--- a/solution.py
+++ b/solution.py
@@ -52,36 +52,27 @@
 
 
 class Place:
-    def __init__(self, shards):
-        self.shards = shards
-        per_plane = shards // 4
+    def __init__(self):
         q = lax.axis_index("seq")
         s = lax.axis_index("shard")
         self.q, self.s = q, s
-        self.core = lax.rem(s, 2)
-        plane, member = s // per_plane, lax.rem(s, per_plane)
-        side = lax.rem(q + plane + member, 2)
-        self.to = (plane, member * 4 + side * 2 + q // 2)
-        group, side_here = s // 4, lax.rem(s // 2, 2)
-        self.quarter = lax.rem(side_here + q + group, 2) + 2 * self.core
-        self.origin = (self.quarter, q * per_plane + group)
-        self.stays = (self.to[0] == q) & (self.to[1] == s)
-        self.sibling = (q, s + 1 - 2 * self.core)
-        self.beside = (q, s + 2 - 4 * side_here)
-        self.quarters = [
-            lax.rem(side_here + j // 2 + q + group, 2) + 2 * (j % 2) for j in range(4)
-        ]
+        self.core = core = lax.rem(s, 2)
+        self.to = (2 * core + lax.rem(q, 2), s - core + q // 2)
+        side = lax.rem(q, 2)
+        self.quarter = side + 2 * core
+        self.origin = (self.quarter, s - core + q // 2)
+        self.stays = q // 2 == core
+        self.sibling = (q, s + 1 - 2 * core)
+        self.beside = (q + 1 - 2 * side, s)
+        self.quarters = [side, side + 2, 1 - side, 3 - side]
 
 
 def relocation(n_seq, shards):
-    per_plane = shards // 4
-    pairs = []
-    for q in range(n_seq):
-        for s in range(shards):
-            plane, member = s // per_plane, s % per_plane
-            side = (q + plane + member) % 2
-            pairs.append((q * shards + s, plane * shards + member * 4 + side * 2 + q // 2))
-    return pairs
+    return [
+        (q * shards + s, (2 * (s % 2) + q % 2) * shards + s - s % 2 + q // 2)
+        for q in range(n_seq)
+        for s in range(shards)
+    ]
 
 
 def remote(src, dst, send, recv, device):
@@ -107,25 +98,30 @@
 
 def forward_kernel(dims, *refs):
     shards, rows, width, heads, gather = dims
-    n_in = 4
-    tok, length_in, w_in, vec_in = refs[:n_in]
-    (ka_o, va_o, kt_o, qat_o, ctxt_o, ctx_o, h1_o, wf_o, xown_o, len_o, vec_o, inb_o) = refs[
-        n_in : n_in + 12
-    ]
+    n_more = 3 if gather else 0
+    tok, length_in, w_in, vec_in = refs[:4]
+    shares = refs[4 : 4 + n_more]
+    refs = refs[4 + n_more :]
+    (ka_o, va_o, kt_o, qat_o, ctxt_o, ctx_o, h1_o, wf_o, xown_o, len_o, vec_o, inb_o) = refs[:12]
+    wholes = refs[12 : 12 + n_more]
+    refs = refs[12 + n_more :]
     (
         xs, wf, vg, lens, h1, ka, va, kt, vt, qat, ctxt, ctx,
         perm_s, perm_r, sib_s, sib_r, side_s, side_r, back_s, back_r,
-        len_s, len_r, w_s, w_r, out_s, ctx_s, ctx_r,
-    ) = refs[n_in + 12 :]
-    here = Place(shards)
+        len_s, len_r, w_s, w_r, out_s, ctx_s, ctx_r, all_s, all_r, all_l,
+    ) = refs
+    here = Place()
     core, s = here.core, here.s
     half = width // 2
     share = width // shards
     chunks = 4
     step = rows // chunks
-    partner_y = (here.q, s + 4 - 8 * lax.rem(s // 4, 2))
-
-    partners = [here.sibling, here.beside] + ([partner_y] if gather else [])
+    x_bit, y_bit = lax.rem(s // 2, 2), lax.rem(s // 4, 2)
+    shard_x, shard_y = s + 2 - 4 * x_bit, s + 4 - 8 * y_bit
+    shard_d = shard_x + 4 - 8 * y_bit
+    partner_x, partner_y = (here.q, shard_x), (here.q, shard_y)
+
+    partners = [here.sibling, here.beside] + ([partner_x, partner_y] if gather else [])
     greet(here, partners, here.origin)
 
     to_core = here.q // 2
@@ -184,16 +180,20 @@
         copy.start()
         w_copies.append(copy)
 
-    def hop(count, device, at):
-        first = s // count * count
-        rows_of = pl.ds(pl.multiple_of(first * share, share), count * share)
-        one = remote(wf.at[rows_of, :], wf.at[rows_of, :], w_s.at[at], w_r.at[at], device)
-        two = remote(
-            vg.at[pl.ds(first, count)], vg.at[pl.ds(first, count)], w_s.at[at + 1], w_r.at[at + 1], device
-        )
-        one.start()
-        two.start()
-        return [one, two]
+    def w_move(at):
+        src, count, device = (
+            (s - core, 2, partner_x),
+            (s - core, 2, partner_y),
+            (shard_x - core, 1, partner_y),
+            (shard_y - core + 1, 1, partner_x),
+        )[at]
+        part = wf.at[pl.ds(pl.multiple_of(src * share, share), count * share), :]
+        return remote(part, part, w_s.at[8 + at], w_r.at[8 + at], device)
+
+    def v_move(at):
+        src, device = ((s, partner_x), (s, partner_y), (shard_x, partner_y))[at]
+        part = vg.at[pl.ds(src - core, 2)]
+        return remote(part, part, w_s.at[12 + at], w_r.at[12 + at], device)
 
     def receive(i):
         pltpu.make_async_copy(tok.at[pl.ds(i * step, step), :], block(xs, core, i), perm_r.at[i]).wait()
@@ -210,18 +210,82 @@
         copy.start()
         return copy
 
+    def rows_of(k, shard):
+        count = shares[k].shape[0]
+        return pl.ds(pl.multiple_of(shard * count, count), count)
+
+    def piece(k, shard, part=None):
+        cut = shares[k].shape[1] // 2
+        if part is None:
+            return wholes[k].at[rows_of(k, shard), :]
+        return wholes[k].at[rows_of(k, shard), part * cut : (part + 1) * cut]
+
+    def pass_on(k, slot, src, dst, device):
+        return remote(src, dst, all_s.at[k, slot], all_r.at[k, slot], device)
+
+    def got(k, slot, ref):
+        pass_on(k, slot, ref, ref, here.sibling).wait_recv()
+
+    def move(k, slot):
+        src, device = (
+            (None, partner_x),
+            (None, partner_y),
+            (None, here.sibling),
+            ((shard_x, 0), partner_y),
+            ((shard_x,), here.sibling),
+            ((shard_y, 1), partner_x),
+            ((shard_y,), here.sibling),
+            ((shard_d,), here.sibling),
+        )[slot]
+        if src is None:
+            return pass_on(k, slot, shares[k], piece(k, s), device)
+        return pass_on(k, slot, piece(k, *src), piece(k, *src), device)
+
+    def share_out(k):
+        for slot in range(3):
+            move(k, slot).start()
+        pltpu.make_async_copy(shares[k], piece(k, s), all_l.at[k]).start()
+
+    def from_x(k):
+        got(k, 0, piece(k, shard_x))
+        move(k, 3).start()
+        move(k, 4).start()
+
+    def from_y(k):
+        got(k, 1, piece(k, shard_y))
+        move(k, 5).start()
+        move(k, 6).start()
+
+    def from_far(k):
+        got(k, 3, piece(k, shard_d, 0))
+        got(k, 5, piece(k, shard_d, 1))
+        move(k, 7).start()
+
+    def all_here(k):
+        flip = 1 - 2 * core
+        for slot, shard in ((2, s), (4, shard_x), (6, shard_y), (7, shard_d)):
+            got(k, slot, piece(k, shard + flip))
+        pltpu.make_async_copy(shares[k], piece(k, s), all_l.at[k]).wait()
+
     moved = []
-    hops = []
     if gather:
         for copy in w_copies:
             copy.wait()
-        hops += hop(2, here.beside, 8)
+        for at in range(2):
+            w_move(at).start()
+            v_move(at).start()
+        for k in range(n_more):
+            share_out(k)
     moved += receive(0)
     moved += receive(1)
     if gather:
-        for copy in hops:
-            copy.wait_recv()
-        second = hop(4, partner_y, 10)
+        w_move(0).wait_recv()
+        v_move(0).wait_recv()
+        w_move(2).start()
+        v_move(2).start()
+        w_move(1).wait_recv()
+        v_move(1).wait_recv()
+        w_move(3).start()
     moved += receive(2)
     moved += receive(3)
 
@@ -235,15 +299,16 @@
         lax.fori_loop(0, count // 256, body, 0)
 
     if gather:
-        for copy in second:
-            copy.wait_recv()
+        w_move(2).wait_recv()
+        w_move(3).wait_recv()
+        v_move(2).wait_recv()
         for i in range(shards):
-            piece = vg[i].astype(F32)
-            vec_o[:, i * share : (i + 1) * share] = piece[:, :share]
+            part = vg[i].astype(F32)
+            vec_o[:, i * share : (i + 1) * share] = part[:, :share]
             for r in range(4):
                 at = (4 * i + r) * share
                 inb_o[:, at : at + share] = jnp.broadcast_to(
-                    piece[IB + r : IB + r + 1, :share], (8, share)
+                    part[IB + r : IB + r + 1, :share], (8, share)
                 )
     else:
         for copy in w_copies:
@@ -300,6 +365,9 @@
     norm_one(0, 2 * rows)
     project(0)
     project(1)
+    if gather:
+        from_x(0)
+        from_y(0)
     relays = [relay(i) for i in range(chunks)]
     for i in range(chunks):
         pl_block = block(xs, 3 - core, i)
@@ -307,6 +375,9 @@
     norm_one(2 * rows, 2 * rows)
     project(2)
     project(3)
+    if gather:
+        from_x(1)
+        from_y(1)
 
     saves = []
     own = pl.ds(pl.multiple_of(core * rows, rows), rows)
@@ -349,6 +420,25 @@
             for r, term in enumerate((high, mid, low)):
                 rest = jnp.where(index == r, term.astype(F32), rest)
             qat[h, 64:80, at] = rest.astype(BF)
+
+        if gather:
+            @pl.when(h == 0)
+            def _():
+                from_far(0)
+
+            @pl.when(h == heads // 3)
+            def _():
+                from_x(2)
+                from_y(2)
+
+            @pl.when(h == heads - 2)
+            def _():
+                from_far(1)
+
+            @pl.when(h == heads - 1)
+            def _():
+                from_far(2)
+
         return 0
 
     lax.fori_loop(0, heads, attend, 0)
@@ -381,11 +471,17 @@
     for copy in moved + relays:
         copy.wait_send()
     if gather:
-        for copy in hops + second:
-            copy.wait_send()
-
-
-def attention_forward(dims, tok, length, w, vec):
+        for k in range(n_more):
+            all_here(k)
+            for slot in range(8):
+                move(k, slot).wait_send()
+        for at in range(4):
+            w_move(at).wait_send()
+        for at in range(3):
+            v_move(at).wait_send()
+
+
+def attention_forward(dims, tok, length, w, vec, *shares):
     shards, rows, width, heads, gather = dims
     half = width // 2
     keys = 4 * rows
@@ -402,13 +498,13 @@
         ((8, 128), jnp.int32),
         ((VROWS, width), F32),
         ((8, 4 * width), F32),
-    ]
+    ] + [((shards * share.shape[0], share.shape[1]), BF) for share in shares]
     sems = pltpu.SemaphoreType.DMA
     return pl.pallas_call(
         functools.partial(forward_kernel, dims),
         out_shape=tuple(jax.ShapeDtypeStruct(*o) for o in out),
-        in_specs=[ANY, VMEM, ANY, VMEM],
-        out_specs=tuple([ANY] * 10 + [VMEM] * 2),
+        in_specs=[ANY, VMEM, ANY, VMEM] + [ANY] * len(shares),
+        out_specs=tuple([ANY] * 10 + [VMEM] * 2 + [ANY] * len(shares)),
         scratch_shapes=[
             pltpu.VMEM((keys, width), BF),
             pltpu.VMEM((width, 3 * half), BF),
@@ -423,21 +519,22 @@
             pltpu.VMEM((half, 2 * rows), BF),
             pltpu.VMEM((width, rows), BF),
             sems((4,)), sems((4,)), sems((4,)), sems((4,)), sems((4,)), sems((4,)), sems((4,)), sems((4,)),
-            sems, sems, sems((12,)), sems((12,)), sems((12,)), sems, sems,
+            sems, sems, sems((16,)), sems((16,)), sems((12,)), sems, sems,
+            sems((3, 8)), sems((3, 8)), sems((3,)),
         ],
         compiler_params=pltpu.CompilerParams(
             collective_id=0, has_side_effects=True, vmem_limit_bytes=56 * 2**20
         ),
         name="attention_forward",
-    )(tok, length, w, vec)
+    )(tok, length, w, vec, *shares)
 
 
 def feed_kernel(dims, *refs):
-    shards, rows, width, heads, _ = dims
+    shards, rows, width, heads, blocked = dims
     ctx, x, cot, lens, vec, inb, wo_h, wi_h, wf_h = refs[:9]
     out_o, ect_o, gmid_o, gwi_o, gwf_o, gwo_o, vec_o, gib_o = refs[9:17]
     wo, wi, wf, mid, h2, h2t, eo, eot, gh2, acc, in_s = refs[17:]
-    here = Place(shards)
+    here = Place()
     loads = []
     for at, (src, dst) in enumerate(((wo_h, wo), (wi_h, wi), (wf_h, wf))):
         copy = pltpu.make_async_copy(src, dst, in_s.at[at])
@@ -467,7 +564,8 @@
     loads[1].wait()
     loads[2].wait()
 
-    size = 512
+    size = width
+    share, half = width // shards, width // 2
 
     def part(c, _):
         at = pl.ds(pl.multiple_of(c * size, size), size)
@@ -482,9 +580,22 @@
         e_inner = (dot_t(eo[...], wfc) * slope).astype(BF)
         acc[...] += dot(active, wfc)
         gh2[...] += dot_t(e_inner, wic)
-        gwf_o[:, at] = dot(eot[...], active).astype(BF)
+        grads = dot(eot[...], active).astype(BF)
+        if blocked:
+            for core in range(2):
+                for ab in range(2):
+                    gwf_o[c // 2, lax.rem(c, 2), core, ab] = grads[
+                        ab * half : (ab + 1) * half, core * half : (core + 1) * half
+                    ]
+        else:
+            gwf_o[:, at] = grads
         grads = dot(h2t[...], e_inner)
-        gwi_o[:, at] = grads[:width].astype(BF)
+        if blocked:
+            to = pl.ds(pl.multiple_of(lax.rem(c, 2) * size, size), size)
+            for i in range(shards):
+                gwi_o[i // 4, i // 2 % 2, i % 2, c // 2, :, to] = grads[i * share : (i + 1) * share].astype(BF)
+        else:
+            gwi_o[:, at] = grads[:width].astype(BF)
         gib_o[:, at] = grads[width : width + 8]
         return 0
 
@@ -501,19 +612,36 @@
     gmid_o[...] = grad_mid
     e_branch = grad_mid.astype(BF)
     vec_o[OB : OB + 1, :] = jnp.sum(e_branch.astype(F32), 0, keepdims=True)
-    gwo_o[...] = dot(ctx[...], e_branch).astype(BF)
+    grads = dot(ctx[...], e_branch).astype(BF)
+    if blocked:
+        for i in range(shards):
+            for ab in range(2):
+                gwo_o[i // 4, i // 2 % 2, i % 2, ab] = grads[
+                    i * share : (i + 1) * share, ab * half : (ab + 1) * half
+                ]
+    else:
+        gwo_o[...] = grads
     ect_o[...] = dot_t(wo[...], e_branch).astype(BF)
+
+
+def grad_blocks(dims):
+    shards, rows, width, heads, blocked = dims
+    if not blocked:
+        return [(width, 4 * width), (width, 4 * width), (width, width)]
+    share, half = width // shards, width // 2
+    return [(2, 2, 2, 2) + part for part in ((half, 4 * share), (share, 2 * width), (share, half))]
 
 
 def feed_forward(dims, ctx, x, cot, lens, vec, inb, wo, wi, wf):
     shards, rows, width, heads, _ = dims
+    blocks = grad_blocks(dims)
     out = [
         ((rows, width), BF),
         ((width, rows), BF),
         ((rows, width), F32),
-        ((width, 4 * width), BF),
-        ((width, 4 * width), BF),
-        ((width, width), BF),
+        (blocks[1], BF),
+        (blocks[0], BF),
+        (blocks[2], BF),
         ((VROWS, width), F32),
         ((8, 4 * width), F32),
     ]
@@ -540,15 +668,164 @@
     )(ctx, x, cot, lens, vec, inb, wo, wi, wf)
 
 
+class Reduction:
+    def __init__(self, here, refs, whole=None):
+        self.mine, self.near, self.got, self.last, self.seq_in, self.done, self.send, self.recv = refs
+        self.here, self.whole = here, whole
+        s, q, core = here.s, here.q, here.core
+        self.x, self.y = lax.rem(s // 2, 2), lax.rem(s // 4, 2)
+        self.side, self.high = lax.rem(q, 2), q // 2
+        self.to_x = (q, s + 2 - 4 * self.x)
+        self.to_y = (q, s + 4 - 8 * self.y)
+        self.to_far = (q + 2 - 4 * self.high, s)
+        self.own = self.mine.at[self.y, self.x]
+
+    @staticmethod
+    def scratch(r, c, core):
+        sems = pltpu.SemaphoreType.DMA
+        return [
+            pltpu.VMEM((2, 2, 2, r, c), BF),
+            pltpu.VMEM((2, 2, 2, r, c) if core else (16, 128), BF),
+            pltpu.VMEM((2, 2, r, c), BF),
+            pltpu.VMEM((2, r, c), BF),
+            pltpu.VMEM((r + r // 2, c), BF),
+            pltpu.VMEM((2, r, c), BF),
+            sems((10,)),
+            sems((9,)),
+        ]
+
+    def quarter(self, ref, which):
+        r = ref.shape[0] // 2
+        return ref.at[pl.ds(pl.multiple_of(which * r, r), r), :]
+
+    def copy(self, at):
+        x, y, side, high, own, done = self.x, self.y, self.side, self.high, self.own, self.done
+        mine, got, last = self.mine, self.got, self.last
+        r = own.shape[1]
+        if at == 0:
+            src, dst, device = self.whole.at[:, :, 1 - self.here.core], self.near, self.here.sibling
+        elif at == 1:
+            src, dst, device = mine.at[:, 1 - x, 0], got.at[0], self.to_x
+        elif at == 2:
+            src, dst, device = mine.at[1 - y, :, 1], got.at[1], self.to_y
+        elif at == 3:
+            src, dst, device = mine.at[1 - y, x, 0], last.at[0], self.to_y
+        elif at == 4:
+            src, dst, device = mine.at[y, 1 - x, 1], last.at[1], self.to_x
+        elif at == 5:
+            src, dst, device = own.at[1 - side], self.seq_in.at[:r, :], self.here.beside
+        elif at == 6:
+            src, dst, device = self.quarter(own.at[side], 1 - high), self.seq_in.at[r:, :], self.to_far
+        elif at == 7:
+            src = dst = self.quarter(done.at[side], high)
+            device = self.to_far
+        else:
+            src = dst = done.at[side]
+            device = self.here.beside
+        return remote(src, dst, self.send.at[at], self.recv.at[at], device)
+
+    def load(self):
+        return pltpu.make_async_copy(self.whole.at[:, :, self.here.core], self.mine, self.send.at[9])
+
+    def arrived(self, at):
+        done, side, high = self.done, self.side, self.high
+        if at == 7:
+            ref = self.quarter(done.at[side], 1 - high)
+        elif at == 8:
+            ref = done.at[1 - side]
+        else:
+            self.copy(at).wait_recv()
+            return
+        remote(ref, ref, self.send.at[at], self.recv.at[at], self.here.beside).wait_recv()
+
+    def add(self, into, other, out=None):
+        r = into.shape[-2]
+        step = 96 if into.shape[-1] > 512 and r % 96 == 0 else r
+        out = into if out is None else out
+
+        def body(i, _):
+            at = pl.ds(pl.multiple_of(i * step, step), step)
+            out[at, :] = into[at, :] + other[at, :]
+            return 0
+
+        lax.fori_loop(0, r // step, body, 0)
+
+    def phase(self, number):
+        x, y = self.x, self.y
+        if number == 0:
+            self.load().start()
+            self.copy(0).start()
+        elif number == 1:
+            if self.whole is not None:
+                self.load().wait()
+                self.arrived(0)
+                for j in range(2):
+                    for i in range(2):
+                        for ab in range(2):
+                            self.add(self.mine.at[j, i, ab], self.near.at[j, i, ab])
+            self.copy(1).start()
+            self.copy(2).start()
+        elif number == 2:
+            self.arrived(1)
+            self.arrived(2)
+            for i in range(2):
+                self.add(self.mine.at[i, x, 0], self.got.at[0, i])
+                self.add(self.mine.at[y, i, 1], self.got.at[1, i])
+            self.copy(3).start()
+            self.copy(4).start()
+        elif number == 3:
+            self.arrived(3)
+            self.arrived(4)
+            for ab in range(2):
+                self.add(self.own.at[ab], self.last.at[ab])
+            self.copy(5).start()
+        elif number == 4:
+            self.arrived(5)
+            self.add(self.own.at[self.side], self.seq_in)
+            self.copy(6).start()
+        elif number == 5:
+            self.arrived(6)
+            r = self.own.shape[1]
+            self.add(
+                self.quarter(self.own.at[self.side], self.high),
+                self.seq_in.at[r:, :],
+                self.quarter(self.done.at[self.side], self.high),
+            )
+            self.copy(7).start()
+        elif number == 6:
+            self.arrived(7)
+            self.copy(8).start()
+        elif number == 7:
+            self.arrived(8)
+
+    def finish(self):
+        for at in range(0 if self.whole is not None else 1, 9):
+            self.copy(at).wait_send()
+
+
 def backward_kernel(dims, *refs):
-    shards, rows, width, heads, _ = dims
+    shards, rows, width, heads, gather = dims
     ect, ka_h, va_h, kt_h, qat_h, ctxt_h, h1_h, wf_h, x, gmid, vec = refs[:11]
-    gtok_o, gw_o, vec_o = refs[11:14]
+    refs = refs[11:]
+    if gather:
+        vec_two, gib = refs[:2]
+        wholes = refs[2:5]
+        gtok_o, vec_o = refs[5:7]
+        sums_o = refs[7:11]
+        refs = refs[11:]
+    else:
+        gtok_o, gw_o, vec_o = refs[:3]
+        refs = refs[3:]
     (
         ka, va, kt, qat, ctxt, h1, wf, dot_all, doat, grads, dk_sum, dv_sum, sib_out, sib_in, side_out, side_in,
         own_sum, gt, load_s, do_s, do_r, sib_s, sib_r, side_s, side_r, perm_s, perm_r,
-    ) = refs[14:]
-    here = Place(shards)
+    ) = refs[:27]
+    refs = refs[27:]
+    here = Place()
+    if gather:
+        sums = [Reduction(here, refs[8 * i : 8 * i + 8], wholes[i]) for i in range(3)]
+        sums.append(Reduction(here, refs[24:32]))
+        gw_o, trade_in, trade_s, trade_r, vec_in, vec_s, vec_r, final_s = refs[32:]
     core = here.core
     half = width // 2
     keys = 4 * rows
@@ -563,7 +840,17 @@
         copy.start()
         loads.append(copy)
 
-    greet(here, [here.sibling, here.beside], here.to)
+    partners = [here.sibling, here.beside]
+    if gather:
+        partners += [sums[0].to_x, sums[0].to_y, sums[0].to_far]
+    greet(here, partners, here.to)
+
+    def run(*steps):
+        if gather:
+            for which, number in steps:
+                sums[which].phase(number)
+
+    run((0, 0), (1, 0), (2, 0))
 
     mine = pl.ds(pl.multiple_of(core * half, 128), half)
     theirs = pl.ds(pl.multiple_of((1 - core) * half, 128), half)
@@ -617,6 +904,12 @@
                     grads[pl.ds(pl.multiple_of(half + h * 64, 64), 64), to] = e_key.astype(BF)
                     grads[pl.ds(pl.multiple_of(2 * half + h * 64, 64), 64), to] = e_value.astype(BF)
             grads[head, at] = (e_query * HEAD_DIM**-0.5).astype(BF)
+
+        for when, steps in IN_HEADS:
+            @pl.when(h == when)
+            def _():
+                run(*steps)
+
         return 0
 
     lax.fori_loop(0, heads, attend, 0)
@@ -639,6 +932,7 @@
         copy = remote(side_out.at[:, at], side_in.at[:, at], side_s.at[i], side_r.at[i], here.beside)
         copy.start()
         sides.append(copy)
+    run(*TAIL[0])
     sib_out[1] = partial_of(1 - core, True).astype(BF)
     near = remote(sib_out.at[1], sib_in.at[1], sib_s.at[1], sib_r.at[1], here.sibling)
     near.start()
@@ -646,9 +940,18 @@
     near.wait_recv()
     own_sum[...] = own_part + sib_in[1].astype(F32)
 
-    gw_o[:, :half] = dot(grads[:half, : 2 * rows], h1[: 2 * rows, :]).T.astype(BF)
-    gw_o[:, half : 2 * half] = dot(grads[half : 2 * half, :], h1[...]).T.astype(BF)
-    gw_o[:, 2 * half :] = dot(grads[2 * half :, :], h1[...]).T.astype(BF)
+    for i, (left, right) in enumerate(
+        ((grads[:half, : 2 * rows], h1[: 2 * rows, :]), (grads[half : 2 * half, :], h1[...]), (grads[2 * half :, :], h1[...]))
+    ):
+        result = dot(left, right).T.astype(BF)
+        at = slice(i * half, (i + 1) * half)
+        if gather:
+            share = width // shards
+            for j in range(shards):
+                sums[3].mine[j // 4, j // 2 % 2, j % 2, :, at] = result[j * share : (j + 1) * share]
+        else:
+            gw_o[:, at] = result
+    run(*TAIL[1])
     vec_o[...] = jnp.zeros_like(vec_o)
 
     def row_sums(values):
@@ -658,8 +961,10 @@
             folded += values[:, i * 128 : (i + 1) * 128].astype(F32)
         return jnp.sum(folded.T, 0, keepdims=True)
 
-    vec_o[QB : QB + 1, :half] = row_sums(grads[:half, : 2 * rows])
-    vec_o[VB : VB + 1, :half] = row_sums(grads[2 * half :, :])
+    for at, part in ((QB, grads[:half, : 2 * rows]), (VB, grads[2 * half :, :])):
+        total = row_sums(part)
+        for i in range(2):
+            vec_o[at : at + 1, i * half : (i + 1) * half] = jnp.where(core == i, total, 0.0)
 
     gain = vec[LN1G : LN1G + 1, :]
 
@@ -698,6 +1003,44 @@
     vec_o[LN1G : LN1G + 1, :] = gain_sum
     vec_o[LN1B : LN1B + 1, :] = shift_sum
 
+    if gather:
+        vec_o[OB:IB, :] = vec_two[OB:IB, :]
+        for r in range(4):
+            vec_o[IB + r : IB + r + 1, :] = gib[0:1, r * width : (r + 1) * width]
+        steps = [here.sibling, here.beside, sums[0].to_x, sums[0].to_y, sums[0].to_far]
+        vec_copies = []
+        for i, device in enumerate(steps):
+            src = vec_o if i == 0 else vec_in.at[2 * i - 1]
+            copy = remote(src, vec_in.at[2 * i], vec_s.at[i], vec_r.at[i], device)
+            copy.start()
+            vec_copies.append(copy)
+            run(*TAIL[2 + i])
+            copy.wait_recv()
+            if i < 4:
+                vec_in[2 * i + 1] = src[...] + vec_in[2 * i]
+            else:
+                for last in vec_copies:
+                    last.wait_send()
+                vec_o[...] = src[...] + vec_in[2 * i]
+        run(*TAIL[7])
+        trade_w = remote(sums[3].done.at[1 - core], trade_in, trade_s, trade_r, here.sibling)
+        trade_w.start()
+        finals = []
+        for i in range(3):
+            copy = pltpu.make_async_copy(sums[i].done, sums_o[i], final_s.at[i])
+            copy.start()
+            finals.append(copy)
+        trade_w.wait()
+        for i, src in enumerate((sums[3].done.at[core], trade_in)):
+            which = core if i == 0 else 1 - core
+            copy = pltpu.make_async_copy(src, sums_o[3].at[which], final_s.at[3 + i])
+            copy.start()
+            finals.append(copy)
+        for copy in finals:
+            copy.wait()
+        for each in sums:
+            each.finish()
+
     for copy in [away, near] + sides:
         copy.wait_send()
     for i in range(chunks):
@@ -709,17 +1052,53 @@
             perm_copy(i).wait_send()
 
 
+IN_HEADS = (
+    (0, ((0, 1),)),
+    (2, ((1, 1),)),
+    (3, ((0, 2),)),
+    (4, ((0, 3), (2, 1))),
+    (5, ((1, 2), (0, 4))),
+)
+TAIL = (
+    ((0, 5),),
+    ((3, 1), (1, 3), (2, 2), (0, 6)),
+    ((2, 3), (1, 4)),
+    ((3, 2), (1, 5)),
+    ((3, 3), (2, 4), (1, 6)),
+    ((3, 4), (2, 5)),
+    ((3, 5), (2, 6), (0, 7), (1, 7)),
+    ((3, 6), (2, 7), (3, 7)),
+)
+
+
 def attention_backward(dims, *args):
-    shards, rows, width, heads, _ = dims
+    shards, rows, width, heads, gather = dims
     half = width // 2
     keys = 4 * rows
-    out = [((rows, width), BF), ((width, 3 * half), BF), ((VROWS, width), F32)]
+    share = width // shards
     sems = pltpu.SemaphoreType.DMA
+    if gather:
+        parts = [block[4:] for block in grad_blocks(dims)]
+        out = [((rows, width), BF), ((VROWS, width), F32)]
+        out += [((2,) + part, BF) for part in parts] + [((2, share, 3 * half), BF)]
+        in_specs = [VMEM] + [ANY] * 7 + [VMEM] * 5 + [ANY] * 3
+        out_specs = (ANY, VMEM) + (ANY,) * 4
+        more = sum((Reduction.scratch(*part, True) for part in parts), [])
+        more += Reduction.scratch(share, 3 * half, False)
+        more += [
+            pltpu.VMEM((16, 128), BF), pltpu.VMEM((share, 3 * half), BF), sems, sems,
+            pltpu.VMEM((9, VROWS, width), F32), sems((5,)), sems((5,)), sems((5,)),
+        ]
+    else:
+        out = [((rows, width), BF), ((width, 3 * half), BF), ((VROWS, width), F32)]
+        in_specs = [VMEM] + [ANY] * 7 + [VMEM] * 3
+        out_specs = (ANY, VMEM, VMEM)
+        more = []
     return pl.pallas_call(
         functools.partial(backward_kernel, dims),
         out_shape=tuple(jax.ShapeDtypeStruct(*o) for o in out),
-        in_specs=[VMEM] + [ANY] * 7 + [VMEM] * 3,
-        out_specs=(ANY, VMEM, VMEM),
+        in_specs=in_specs,
+        out_specs=out_specs,
         scratch_shapes=[
             pltpu.VMEM((heads, keys, 128), BF),
             pltpu.VMEM((heads, keys, 128), BF),
@@ -740,9 +1119,9 @@
             pltpu.VMEM((width, rows), F32),
             pltpu.VMEM((rows, width), BF),
             sems((7,)), sems((2,)), sems, sems((2,)), sems((2,)), sems((4,)), sems((4,)), sems((4,)), sems((4,)),
-        ],
+        ] + more,
         compiler_params=pltpu.CompilerParams(
-            collective_id=1, has_side_effects=True, vmem_limit_bytes=58 * 2**20
+            collective_id=1, has_side_effects=True, vmem_limit_bytes=60 * 2**20
         ),
         name="attention_backward",
     )(*args)
@@ -777,45 +1156,45 @@
         w_here = lax.dynamic_index_in_dim(
             full_w.reshape(width, 3, 2, half), core, 2, keepdims=False
         ).reshape(width, 3 * half)
-    (ka, va, kt, qat, ctxt, ctx, h1, wf, x, lens, vecs, inb) = attention_forward(
-        dims, tokens.reshape(rows, width), length, w_here, vec
+    shares = (w_out, w_in, w_fin) if gather else ()
+    (ka, va, kt, qat, ctxt, ctx, h1, wf, x, lens, vecs, inb, *wholes) = attention_forward(
+        dims, tokens.reshape(rows, width), length, w_here, vec, *shares
     )
     if not gather:
         inb = jnp.broadcast_to(
             lax.all_gather(in_bias, "shard", axis=0, tiled=True).astype(F32)[None], (8, 4 * width)
         )
-    full_wo = lax.all_gather(w_out, "shard", axis=0, tiled=True)
-    full_wi = lax.all_gather(w_in, "shard", axis=0, tiled=True)
-    full_wf = lax.all_gather(w_fin, "shard", axis=0, tiled=True)
+        wholes = [lax.all_gather(w, "shard", axis=0, tiled=True) for w in (w_out, w_in, w_fin)]
     cot = lax.ppermute(cotangent.reshape(rows, width), axes, there)
     out, ect, gmid, gwi, gwf, gwo, vec_two, gib = feed_forward(
-        dims, ctx, x, cot, lens, vecs, inb, full_wo, full_wi, full_wf
+        dims, ctx, x, cot, lens, vecs, inb, *wholes
     )
     output = lax.ppermute(out, axes, back).reshape(tokens.shape)
-    gtok, gw, vec_one = attention_backward(
-        dims, ect, ka, va, kt, qat, ctxt, h1, wf, x, gmid, vecs
-    )
-
-    def total(grad, dim):
-        part = lax.psum_scatter(grad, "shard", scatter_dimension=dim, tiled=True)
-        return lax.psum(part, "seq").astype(F32)
-
-    total_wi = total(gwi, 0)
-    total_wf = total(gwf, 1).T
-    total_wo = total(gwo, 0)
-    wide = jnp.zeros((width, 3, 2, half), BF)
-    wide = lax.dynamic_update_index_in_dim(wide, gw.reshape(width, 3, half), core, 2)
-    total_w = total(wide.reshape(width, 3 * width), 0)
-
-    halves = jnp.zeros((2, 2, half), F32)
-    halves = lax.dynamic_update_index_in_dim(halves, vec_one[QB : VB + 1, :half], core, 1).reshape(2, width)
-    sums = jnp.concatenate(
-        (vec_one[:QB], halves, vec_two[OB:IB], gib[0].reshape(4, width))
-    )
-    sums = lax.psum(sums, axes)
+    args = (ect, ka, va, kt, qat, ctxt, h1, wf, x, gmid, vecs)
     s = lax.axis_index("shard")
+    if gather:
+        gtok, sums, t_wf, t_wi, t_wo, t_w = attention_backward(dims, *args, vec_two, gib, gwf, gwi, gwo)
+        total_wf = t_wf.reshape(width, 4 * share).T.astype(F32)
+        total_wi = t_wi.transpose(1, 0, 2).reshape(share, 4 * width).astype(F32)
+        total_wo = t_wo.transpose(1, 0, 2).reshape(share, width).astype(F32)
+        total_w = t_w.reshape(2, share, 3, half).transpose(1, 2, 0, 3).reshape(share, 3 * width).astype(F32)
+    else:
+        gtok, gw, vec_one = attention_backward(dims, *args)
+
+        def total(grad, dim):
+            part = lax.psum_scatter(grad, "shard", scatter_dimension=dim, tiled=True)
+            return lax.psum(part, "seq").astype(F32)
+
+        total_wi = total(gwi, 0)
+        total_wf = total(gwf, 1).T
+        total_wo = total(gwo, 0)
+        wide = jnp.zeros((width, 3, 2, half), BF)
+        wide = lax.dynamic_update_index_in_dim(wide, gw.reshape(width, 3, half), core, 2)
+        total_w = total(wide.reshape(width, 3 * width), 0)
+        sums = jnp.concatenate((vec_one[:OB], vec_two[OB:IB], gib[0].reshape(4, width)))
+        sums = lax.psum(sums, axes)
     mine = lax.dynamic_slice_in_dim(sums[:IB], s * share, share, 1)
-    total_ib = lax.dynamic_slice_in_dim(sums[IB:].reshape(-1), s * 4 * share, 4 * share, 0)
+    total_ib = lax.dynamic_slice_in_dim(sums[IB:VECS].reshape(-1), s * 4 * share, 4 * share, 0)
     return (
         output,
         gtok.reshape(tokens.shape),

time: 604 us -> 295 us (0.49)
  waiting for transfers between devices: 143 us -> 13.6 us
  local copies, waits for them, and re-layouts: 91.6 us -> 15.1 us
  blocking collectives: 65.8 us -> 0 us
  Pallas kernels: 268 us -> 252 us
  between operations: 15 us -> 1.43 us
    reduce_scatter x3 -> x0, waiting for transfers between devices: 102 us -> none  [total(): part = lax.psum_scatter(grad, 'shard', scatter_dimension=dim, tiled=True)]
    psum x1 -> x0, blocking collectives: 65.8 us -> none  [on_device(): sums = lax.psum(sums, axes)]
    pallas_call x1, Pallas kernels: 142 us -> 82.4 us  [attention_forward(): pl.pallas_call(functools.partial(forward_kernel, dims), out_shape=tuple((...]
    dynamic_update_slice x2 -> x0, local copies, waits for them, and re-layouts: 54.5 us -> none  [the longest x1 54.5 us: on_device(): lax.dynamic_update_index_in_dim(wide, gw.reshape(width, 3, half), core, 2)]
    pallas_call x1, Pallas kernels: 97.9 us -> 142 us  [attention_backward(): pl.pallas_call(functools.partial(backward_kernel, dims), out_shape=tuple(...]
    all_gather x3 -> x0, waiting for transfers between devices: 19.8 us -> none  [the longest x1 19.8 us: on_device(): full_wf = lax.all_gather(w_fin, 'shard', axis=0, tiled=True)]
    psum x1 -> x0, waiting for transfers between devices: 18 us -> none  [total(): return lax.psum(part, 'seq').astype(F32)]
    ppermute x1, waiting for transfers between devices: 0.01 us -> 13.6 us  [on_device(): output = lax.ppermute(out, axes, back).reshape(tokens.shape)]
  transfers between devices with their start and end apart: 10 -> 2, of which waited for: 4 -> 1; matrix products, arithmetic and copies ran while one was open for 14% -> 3% of each run, Pallas kernels for 40% -> 28%
where the time goes in v2:
time: 295 us
  Pallas kernels  252 us (85%)
  local copies, waits for them, and re-layouts  15.1 us (5%)
  waiting for transfers between devices  13.6 us (5%)
  starting transfers between devices  12.1 us (4%)
    pallas_call x1, Pallas kernels, attention_backward(): pl.pallas_call(functools.partial(backward_kernel, dims), out_shape=tuple(...  142 us
    pallas_call x1, Pallas kernels, attention_forward(): pl.pallas_call(functools.partial(forward_kernel, dims), out_shape=tuple((...  82.4 us
    pallas_call x1, Pallas kernels, feed_forward(): pl.pallas_call(functools.partial(feed_kernel, dims), out_shape=tuple((jax...  27.8 us
    ppermute x1, waiting for transfers between devices, on_device(): output = lax.ppermute(out, axes, back).reshape(tokens.shape)  13.6 us
    ppermute x1, starting transfers between devices, on_device(): output = lax.ppermute(out, axes, back).reshape(tokens.shape)  6.5 us
  transfers between devices with their start and end apart: 2, of which 1 were waited for; matrix products, arithmetic and copies ran while one was open for 3% of the time, Pallas kernels for 28%

profile of v2, /device:TPU:1, one launch (start us, length us, event | category | flops | bytes accessed | tf_op | source)
XLA Modules:
  0.0 295.0 jit_solution(14177274602430623380)
XLA Ops:
  0.6 5.6 %collective-permute-start = (bf16[512,768]{1,0:T(8,128)(2,1)}, bf16[512,768]{1,0:T(8,128)(2,1)S(1)}, u32[]{:S(2)}, u32[]{:S(2)}) collective-permute-start(bf16[512,768]{1,0:T(8,128)(2,1)} %bitcast.58), channel_id=1, source_target_pairs={{0,0},{1,16},{2,2},{3,18},{4,4},{5,20},{6,6},{7,22},{8,8},{9,24},{... | collective-permute-start | bytes 2359304 | tf_op jit(solution)/shard_map/ppermute | solution.py:1168
  6.3 0.8 reshape.98
  7.7 0.8 concatenate.3
  8.5 0.6 pad.4.refs_3_
  9.1 0.6 broadcast_in_dim.8.refs_1_
  9.7 82.4 %attention_forward.1 = (bf16[6,2048,128]{2,1,0:T(8,128)(2,1)}, bf16[6,2048,128]{2,1,0:T(8,128)(2,1)}, bf16[6,64,2048]{2,1,0:T(8,128)(2,1)}, bf16[6,128,1024]{2,1...) custom-call(bf16[512,768]{1,0:T(8,128)(2,1)} %bitcast.48, ...), custom_call_target="tpu_custom_call" | custom-call | tf_op jit(solution)/shard_map/attention_forward/pallas_call | solution.py:503
  92.1 0.0 collective-permute-done.refs_2_
  92.1 0.0 copy-start
  92.1 0.9 copy-done
  93.0 27.8 %feed_forward.1 = (bf16[512,768]{1,0:T(8,128)(2,1)}, bf16[768,512]{1,0:T(8,128)(2,1)}, f32[512,768]{1,0:T(8,128)}, bf16[2,2,2,2,96,1536]{5,4,3,2,1,0:T(8,128)(2,...) custom-call(bf16[768,512]{1,0:T(8,128)(2,1)} %get-tuple-element.44.r, ...), custom_call_target="tpu_custom_call" | custom-call | tf_op jit(solution)/shard_map/feed_forward/pallas_call | solution.py:648
  120.8 142.3 %attention_backward.1 = (bf16[512,768]{1,0:T(8,128)(2,1)}, f32[16,768]{1,0:T(8,128)}, bf16[2,384,384]{2,1,0:T(8,128)(2,1)}, bf16[2,96,1536]{2,1,0:T(8,128)(2,1)}...) custom-call(bf16[768,512]{1,0:T(8,128)(2,1)} %get-tuple-element.53.refs_0_, ...), custom_call_target="tpu_custom_call" | custom-call | tf_op jit(solution)/shard_map/attention_backward/pallas_call | solution.py:1097
  263.1 0.7 slice.30
  263.8 0.7 slice.38
  264.6 1.4 reshape.107
  266.0 0.0 copy-start.3
  266.0 0.7 copy.36
  266.7 1.6 reshape.103
  268.3 0.0 copy-start.2
  268.3 0.0 copy-done.3
  268.3 0.1 convert_bitcast_fusion
  268.5 6.5 %collective-permute-start.1 = (bf16[512,768]{1,0:T(8,128)(2,1)}, bf16[512,768]{1,0:T(8,128)(2,1)S(1)}, u32[]{:S(2)}, u32[]{:S(2)}) collective-permute-start(bf16[512,768]{1,0:T(8,128)(2,1)} %get-tuple-element.52), channel_id=1, source_target_pairs={{0,0},{16,1},{2,2},{18,3},{4,4},{20,5},{6,6},{22,7},{8,8},{24,9},{... | collective-permute-start | bytes 2359304 | tf_op jit(solution)/shard_map/ppermute | solution.py:1172
  275.0 0.0 copy-done.2
  275.0 0.1 bitcast_convert_fusion
  275.1 1.4 copy.39
  276.5 0.0 copy-start.4
  276.5 1.1 copy.41
  277.6 0.0 copy-start.1
  277.6 0.0 copy-done.4
  277.6 0.7 copy.40
  278.4 0.7 dynamic_slice.7
  279.0 0.1 constant_dynamic-slice_fusion
  279.1 0.5 slice_bitcast_fusion
  279.7 13.6 %collective-permute-done.1 = bf16[512,768]{1,0:T(8,128)(2,1)S(1)} collective-permute-done((bf16[512,768]{1,0:T(8,128)(2,1)}, bf16[512,768]{1,0:T(8,128)(2,1)S(1)}, u32[]{:S(2)}, u32[]{:S(2)}) %collective-permute-start.1) | collective-permute-done | bytes 786464 | tf_op jit(solution)/shard_map/ppermute | solution.py:1172
  293.3 0.9 copy.45
  294.1 0.0 copy-done.1
  294.1 0.9 copy.46
  (2 shorter events, 0.0 us)
Async XLA Ops:
  0.6 91.5 %collective-permute-start = (bf16[512,768]{1,0:T(8,128)(2,1)}, bf16[512,768]{1,0:T(8,128)(2,1)S(1)}, u32[]{:S(2)}, u32[]{:S(2)}) collective-permute-start(bf16[512,768]{1,0:T(8,128)(2,1)} %bitcast.58), channel_id=1, source_target_pairs={{0,0},{1,16},{2,2},{3,18},{4,4},{5,20},{6,6},{7,22},{8,8},{9,24},{... | collective-permute-start | bytes 2359304 | tf_op jit(solution)/shard_map/ppermute | solution.py:1168
  92.1 0.9 copy-start
  266.0 2.3 copy-start.3
  268.3 6.6 %copy-start.2 = (bf16[2,384,384]{2,1,0:T(8,128)(2,1)S(1)}, bf16[2,384,384]{2,1,0:T(8,128)(2,1)}, u32[]{:S(2)}) copy-start(bf16[2,384,384]{2,1,0:T(8,128)(2,1)} %get-tuple-element.72) | copy-start | bytes 1769476
  268.5 24.8 %collective-permute-start.1 = (bf16[512,768]{1,0:T(8,128)(2,1)}, bf16[512,768]{1,0:T(8,128)(2,1)S(1)}, u32[]{:S(2)}, u32[]{:S(2)}) collective-permute-start(bf16[512,768]{1,0:T(8,128)(2,1)} %get-tuple-element.52), channel_id=1, source_target_pairs={{0,0},{16,1},{2,2},{18,3},{4,4},{20,5},{6,6},{22,7},{8,8},{24,9},{... | collective-permute-start | bytes 2359304 | tf_op jit(solution)/shard_map/ppermute | solution.py:1172
  276.5 1.1 copy-start.4
  277.6 16.5 %copy-start.1 = (bf16[512,768]{1,0:T(8,128)(2,1)S(1)}, bf16[512,768]{1,0:T(8,128)(2,1)}, u32[]{:S(2)}) copy-start(bf16[512,768]{1,0:T(8,128)(2,1)} %get-tuple-element.67) | copy-start | bytes 2359300
